TPU v7x, 512 devices: a whole 4x4x16 slice. The times are simulated.
512 devices in a mesh: kv: 64 (over z, x), head: 8 (over y, core).
Axes of the slice: x: 4, y: 4, z: 16, core: 2. Of those that a mesh axis runs over, the one named last changes fastest.
Arguments:
- query: bfloat16 [8, 64, 128], P(None, 'head'), may hold values from -144 to 144
- key_cache: bfloat16 [8, 8, 24576, 128], P(None, 'head', 'kv'), may hold values from -6 to 6
- value_cache: bfloat16 [8, 8, 24576, 128], P(None, 'head', 'kv'), may hold values from -6 to 6
- lengths: int32 [8], replicated, may hold values from 2 to 24576, as said below
- residual: bfloat16 [8, 8192], P(None, 'kv'), may hold values from -41 to 41
- out_weight: bfloat16 [8192, 8192], P('head', 'kv'), may hold values from -0.0625 to 0.0625
- norm_gain: bfloat16 [8192], P('kv'), may hold values from 0.25 to 1.75
- gate_weight: bfloat16 [8192, 28672], P('kv', 'head'), may hold values from -0.1875 to 0.1875
- up_weight: bfloat16 [8192, 28672], P('kv', 'head'), may hold values from -0.1875 to 0.1875
- down_weight: bfloat16 [28672, 8192], P('head', 'kv'), may hold values from -0.03125 to 0.03125
Outputs:
- mixed: bfloat16 [8, 8192], P(None, 'kv')
Inputs may be any that keep to these rules, and one draw needn't show every extreme that they name: `lengths`: each sequence has 2 to 24576 live slots, the first ones; some sequence has exactly 24576.
All inputs are finite; a program needn't handle non-finite values.
Results may differ from a plain program's by a relative error of at most 0.023.
Values may be sent and summed in bfloat16 or wider, within the bound.
No kernel may reach another device: no remote copies, remote signals or barrier semaphores. Data moves between devices by JAX's collectives and lax.ppermute only.
A program may use at most 64 MiB of HBM per device.

v0:
```python
import math

import jax
import jax.numpy as jnp
from jax import lax
from jax.sharding import PartitionSpec as P


def local(
    query,
    key_cache,
    value_cache,
    lengths,
    residual,
    out_weight,
    norm_gain,
    gate_weight,
    up_weight,
    down_weight,
):
    batch_rows, local_heads, block_len, head_size = key_cache.shape
    group_count = query.shape[1] // local_heads
    queries = query.reshape(batch_rows, local_heads, group_count, head_size)
    scores = jnp.einsum(
        "skgd,sktd->skgt", queries, key_cache, preferred_element_type=jnp.float32
    ) / math.sqrt(head_size)
    offset = lax.axis_index("kv") * block_len
    places = offset + lax.broadcasted_iota(jnp.int32, (batch_rows, block_len), 1)
    is_live = (places < lengths[:, None])[:, None, None, :]
    scores = jnp.where(is_live, scores, -1e30)
    local_top = jnp.max(scores, axis=-1)
    expo = jnp.where(is_live, jnp.exp(scores - local_top[..., None]), 0.0)
    local_total = jnp.sum(expo, axis=-1)
    numerator = jnp.einsum(
        "skgt,sktd->skgd",
        expo.astype(jnp.bfloat16),
        value_cache,
        preferred_element_type=jnp.float32,
    )
    highest = lax.pmax(local_top, "kv")
    factor = jnp.exp(local_top - highest)
    numerator, denominator = lax.psum((numerator * factor[..., None], local_total * factor), "kv")
    attended = (numerator / denominator[..., None]).reshape(batch_rows, -1).astype(jnp.bfloat16)
    projected = lax.psum(jnp.dot(attended, out_weight, preferred_element_type=jnp.float32), "head")
    hidden_state = residual.astype(jnp.float32) + projected
    width_all = hidden_state.shape[1] * lax.axis_size("kv")
    squares = lax.psum(jnp.sum(hidden_state * hidden_state, axis=1), "kv")
    scale_row = lax.rsqrt(squares / width_all + 1e-05)
    normed = (hidden_state * scale_row[:, None] * norm_gain.astype(jnp.float32)[None, :]).astype(
        jnp.bfloat16
    )
    stacked = jnp.stack(
        [
            jnp.dot(normed, gate_weight, preferred_element_type=jnp.float32),
            jnp.dot(normed, up_weight, preferred_element_type=jnp.float32),
        ]
    )
    summed = lax.psum(stacked, "kv")
    activated = (jax.nn.silu(summed[0]) * summed[1]).astype(jnp.bfloat16)
    downward = lax.psum(jnp.dot(activated, down_weight, preferred_element_type=jnp.float32), "head")
    return (hidden_state + downward).astype(jnp.bfloat16)


def solution(mesh):
    return jax.shard_map(
        local,
        mesh=mesh,
        in_specs=(
            P(None, "head", None),
            P(None, "head", "kv", None),
            P(None, "head", "kv", None),
            P(),
            P(None, "kv"),
            P("head", "kv"),
            P("kv"),
            P("kv", "head"),
            P("kv", "head"),
            P("head", "kv"),
        ),
        out_specs=P(None, "kv"),
        check_vma=False,
    )
```

profile of v0, /device:TPU:1, one launch (start us, length us, event | category | flops | bytes accessed | tf_op | source)
XLA Modules:
  0.0 860.7 jit_solution(2266346249394160942)
XLA Ops:
  6.5 0.0 copy-start
  6.6 0.9 broadcast_compare_fusion
  7.4 1.6 fusion.23
  9.0 122.6 %pmax.7 = f32[8,1,8]{2,0,1:T(8,128)S(1)} all-reduce(f32[8,1,8]{2,0,1:T(8,128)S(1)} %bitcast.51), channel_id=1, replica_groups=mesh['kv'=64,'head'=8] {'kv'}, use_global_device_ids=true, to_apply=%region_1.2 | all-reduce | flops 64 | bytes 512 | tf_op jit(solution)/shard_map/pmax | solution.py:40
  131.6 0.2 fusion.6
  131.8 0.0 copy-start.4
  131.8 0.0 copy-start.5
  131.8 0.0 copy-start.7
  131.8 0.3 fusion.1
  132.1 219.9 %all-reduce = (f32[8,1,8,128]{3,2,0,1:T(8,128)S(1)}, f32[8,8]{1,0:T(8,128)S(1)}) all-reduce(f32[8,1,8,128]{3,2,0,1:T(8,128)S(1)} %fusion.1, f32[8,8]{1,0:T(8,128)S(1)} %get-tuple-element.7), channel_id=1, replica_groups=mesh['kv'=64,'head'=8] {'kv'}, use_global_device_ids=true, to_apply=%region_2.3 | all-reduce | flops 8256 | bytes 66048 | tf_op jit(solution)/shard_map/psum | solution.py:42
  352.0 0.1 fusion.18
  352.1 0.1 fusion.15
  352.2 94.7 %psum.44 = f32[8,128]{1,0:T(8,128)S(1)} all-reduce(f32[8,128]{1,0:T(8,128)S(1)} %fusion.15), channel_id=1, replica_groups=mesh['kv'=64,'head'=8] {'head'}, use_global_device_ids=true, to_apply=%region_5.6 | all-reduce | flops 1024 | bytes 8192 | tf_op jit(solution)/shard_map/psum | solution.py:44
  447.0 0.1 multiply_reduce_fusion
  447.1 110.9 %psum.45 = f32[8]{0:T(128)S(1)} all-reduce(f32[8]{0:T(128)S(1)} %multiply_reduce_fusion), channel_id=1, replica_groups=mesh['kv'=64,'head'=8] {'kv'}, use_global_device_ids=true, to_apply=%region_7.8 | all-reduce | flops 8 | bytes 64 | tf_op jit(solution)/shard_map/psum | solution.py:47
  558.0 0.1 multiply_convert_fusion
  558.1 0.2 convolution_bitcast_fusion
  558.3 0.2 convolution_bitcast_fusion.1
  558.6 0.7 pad_maximum_fusion
  559.3 0.0 all-reduce.3.cloned.1.call-update
  559.3 270.4 %all-reduce.3.cloned.1.call-done = f32[2,8,3584]{2,1,0:T(8,128)} async-done(((f32[2,8,3584]{2,1,0:T(8,128)}), f32[2,8,3584]{2,1,0:T(8,128)}) %all-reduce.3.cloned.1.call-update) | async-done | bytes 229392 | tf_op jit(solution)/shard_map/psum | solution.py:58
  829.7 1.2 fusion.8
  830.9 22.3 %psum.47 = f32[8,128]{1,0:T(8,128)S(1)} all-reduce(f32[8,128]{1,0:T(8,128)S(1)} %fusion.8), channel_id=1, replica_groups=mesh['kv'=64,'head'=8] {'head'}, use_global_device_ids=true, to_apply=%region_9.10 | all-reduce | flops 1024 | bytes 8192 | tf_op jit(solution)/shard_map/psum | solution.py:60
  853.2 0.6 add_convert_fusion
  (17 shorter events, 0.1 us)
Async XLA Ops:
  6.5 551.6 %copy-start = (bf16[128,3584]{1,0:T(8,128)(2,1)S(1)}, bf16[128,3584]{1,0:T(8,128)(2,1)}, u32[]{:S(2)}) copy-start(bf16[128,3584]{1,0:T(8,128)(2,1)} %param.18) | copy-start | bytes 2752516
  6.5 0.9 copy-start.6
  6.5 125.3 %copy-start.3 = (bf16[8,1,384,128]{3,2,1,0:T(8,128)(2,1)S(1)}, bf16[8,1,384,128]{3,2,1,0:T(8,128)(2,1)}, u32[]{:S(2)}) copy-start(bf16[8,1,384,128]{3,2,1,0:T(8,128)(2,1)} %param.12) | copy-start | bytes 2359300
  6.5 823.2 %all-reduce.3.cloned.1.call-start = ((), (), s32[]{:S(2)}) async-start(), calls=%async_computation | async-start | bytes 458752 | tf_op jit(solution)/shard_map/psum | solution.py:58
  131.8 220.3 %copy-start.4 = (bf16[1024,128]{1,0:T(8,128)(2,1)S(1)}, bf16[1024,128]{1,0:T(8,128)(2,1)}, u32[]{:S(2)}) copy-start(bf16[1024,128]{1,0:T(8,128)(2,1)} %param.15) | copy-start | bytes 786436
  131.8 315.2 %copy-start.5 = (bf16[8,128]{1,0:T(8,128)(2,1)S(1)}, bf16[8,128]{1,0:T(8,128)(2,1)}, u32[]{:S(2)}) copy-start(bf16[8,128]{1,0:T(8,128)(2,1)} %param.14) | copy-start | bytes 6148
  131.8 315.3 %copy-start.7 = (bf16[128]{0:T(256)(128)(2,1)S(1)}, bf16[128]{0:T(256)(128)(2,1)}, u32[]{:S(2)}) copy-start(bf16[128]{0:T(256)(128)(2,1)} %param.16) | copy-start | bytes 772
  132.1 426.2 %copy-start.1 = (bf16[128,3584]{1,0:T(8,128)(2,1)S(1)}, bf16[128,3584]{1,0:T(8,128)(2,1)}, u32[]{:S(2)}) copy-start(bf16[128,3584]{1,0:T(8,128)(2,1)} %param.17) | copy-start | bytes 2752516
  558.3 271.4 %copy-start.2 = (bf16[3584,128]{1,0:T(8,128)(2,1)S(1)}, bf16[3584,128]{1,0:T(8,128)(2,1)}, u32[]{:S(2)}) copy-start(bf16[3584,128]{1,0:T(8,128)(2,1)} %param.19) | copy-start | bytes 2752516
Sparse Core Ops, SparseCore 0:
  559.5 270.2 all-reduce.2
where the time goes:
time: 861 us
  blocking collectives  570 us (66%)
  waiting for transfers between devices  270 us (31%)
  between operations  13.5 us (2%)
    psum x1, waiting for transfers between devices, local(): summed = lax.psum(stacked, 'kv')  270 us
    psum x1, blocking collectives, local(): lax.psum((numerator * factor[..., None], local_total * factor), 'kv')  220 us
    pmax x1, blocking collectives, local(): highest = lax.pmax(local_top, 'kv')  123 us
    psum x1, blocking collectives, local(): squares = lax.psum(jnp.sum(hidden_state * hidden_state, axis=1), 'kv')  111 us
    psum x1, blocking collectives, local(): lax.psum(jnp.dot(attended, out_weight, preferred_element_type=jnp.float32...  94.7 us
    psum x1, blocking collectives, local(): lax.psum(jnp.dot(activated, down_weight, preferred_element_type=jnp.float...  22.3 us
  transfers between devices with their start and end apart: 1, of which 1 were waited for; matrix products, arithmetic and copies ran while one was open for 0% of the time, Pallas kernels for 0%

commit v1 on v0

v1 whole, which is shorter than its diff:
```python
import math

import jax
import jax.numpy as jnp
from jax import lax
from jax.sharding import Mesh
from jax.sharding import PartitionSpec as P

KV = ("z", "x")
HEAD = ("y", "core")
NZ, NX, NY, NC = 16, 4, 4, 2
NEG = -1e30


def pieces(value):
    high = lax.reduce_precision(value, 8, 7)
    rest = value - high
    middle = lax.reduce_precision(rest, 8, 7)
    low = rest - middle
    return [high.astype(jnp.bfloat16), middle.astype(jnp.bfloat16), low.astype(jnp.bfloat16)]


def exchange(block, axis, count):
    return lax.all_to_all(jnp.broadcast_to(block[None], (count,) + block.shape), axis, 0, 0)


def merge(outs, logs, axis, count):
    rows = jnp.zeros((16, 128), jnp.bfloat16)
    rows = rows.at[0:3, 0:64].set(jnp.stack(pieces(logs)))
    got = exchange(jnp.concatenate([outs.astype(jnp.bfloat16), rows]), axis, count)
    logs = jnp.sum(got[:, 64:67, 0:64].astype(jnp.float32), axis=1)
    top = jnp.max(logs, axis=0)
    share = jnp.exp(logs - top)
    total = jnp.sum(share, axis=0)
    outs = jnp.sum(got[:, 0:64].astype(jnp.float32) * (share / total)[:, :, None], axis=0)
    return outs, top + jnp.log(total)


def local(
    query,
    key_cache,
    value_cache,
    lengths,
    residual,
    out_weight,
    norm_gain,
    gate_weight,
    up_weight,
    down_weight,
):
    batch_rows, _, block_len, head_size = key_cache.shape
    me = lax.axis_index(KV)
    scores = jnp.einsum(
        "sgd,std->sgt", query, key_cache[:, 0], preferred_element_type=jnp.float32
    ) / math.sqrt(head_size)
    places = me * block_len + lax.broadcasted_iota(jnp.int32, (batch_rows, block_len), 1)
    is_live = (places < lengths[:, None])[:, None, :]
    scores = jnp.where(is_live, scores, NEG)
    top = jnp.max(scores, axis=-1)
    expo = jnp.where(is_live, jnp.exp(scores - top[..., None]), 0.0)
    total = jnp.sum(expo, axis=-1)
    outs = jnp.einsum(
        "sgt,std->sgd",
        expo.astype(jnp.bfloat16),
        value_cache[:, 0],
        preferred_element_type=jnp.float32,
    )
    any_live = total > 0
    outs = outs / jnp.where(any_live, total, 1.0)[..., None]
    logs = jnp.where(any_live, top + jnp.log(jnp.where(any_live, total, 1.0)), NEG)
    outs, logs = outs.reshape(64, 128), logs.reshape(64)
    outs, logs = merge(outs, logs, "z", NZ)
    outs, logs = merge(outs, logs, "x", NX)
    attended = outs.reshape(batch_rows, 1024).astype(jnp.bfloat16)
    projected = jnp.dot(attended, out_weight, preferred_element_type=jnp.float32)
    projected = jnp.sum(exchange(projected, HEAD, NY * NC), axis=0)
    hidden_state = residual.astype(jnp.float32) + projected
    squares = jnp.sum(hidden_state * hidden_state, axis=1)
    scaled = (hidden_state * norm_gain.astype(jnp.float32)[None, :]).astype(jnp.bfloat16)
    gate = jnp.dot(scaled, gate_weight, preferred_element_type=jnp.float32)
    up = jnp.dot(scaled, up_weight, preferred_element_type=jnp.float32)
    tiles = jnp.concatenate([gate, up], axis=1).astype(jnp.bfloat16)
    tiles = tiles.reshape(batch_rows, 56, 128).transpose(1, 0, 2)
    extra = jnp.zeros((8, 8, 128), jnp.bfloat16)
    extra = extra.at[0, :, 0:3].set(jnp.stack(pieces(squares), axis=1))
    terms = lax.all_to_all(jnp.concatenate([tiles, extra]), KV, 0, 0)
    summed = jnp.sum(terms.astype(jnp.float32), axis=0)
    special = jnp.zeros((8, 128), jnp.bfloat16)
    special = special.at[:, 0:3].set(jnp.stack(pieces(jnp.sum(summed[:, 0:3], axis=1)), axis=1))
    got = exchange(jnp.where(me == 56, special, summed.astype(jnp.bfloat16)), KV, NZ * NX)
    squares = jnp.sum(got[56, :, 0:3].astype(jnp.float32), axis=1)
    scale_row = lax.rsqrt(squares / 8192 + 1e-05)
    whole = got[0:56].astype(jnp.float32) * scale_row[None, :, None]
    activated = (jax.nn.silu(whole[0:28]) * whole[28:56]).astype(jnp.bfloat16)
    activated = activated.transpose(1, 0, 2).reshape(batch_rows, 3584)
    downward = jnp.dot(activated, down_weight, preferred_element_type=jnp.float32)
    downward = jnp.sum(exchange(downward, HEAD, NY * NC), axis=0)
    return (hidden_state + downward).astype(jnp.bfloat16)


def solution(mesh):
    fine = Mesh(mesh.devices.reshape(NZ, NX, NY, NC), KV + HEAD)
    return jax.shard_map(
        local,
        mesh=fine,
        in_specs=(
            P(None, HEAD, None),
            P(None, HEAD, KV, None),
            P(None, HEAD, KV, None),
            P(),
            P(None, KV),
            P(HEAD, KV),
            P(KV),
            P(KV, HEAD),
            P(KV, HEAD),
            P(HEAD, KV),
        ),
        out_specs=P(None, KV),
        check_vma=False,
    )
```

time: 861 us -> 119 us (0.14)
  blocking collectives: 570 us -> 71 us
  waiting for transfers between devices: 270 us -> 19 us
  starting transfers between devices: 0.01 us -> 19.8 us
  between operations: 13.5 us -> 0.26 us
    psum x4 -> x0, blocking collectives: 448 us -> none  [the longest x1 220 us: local(): lax.psum((numerator * factor[..., None], local_total * factor), 'kv')]
    psum x1 -> x0, waiting for transfers between devices: 270 us -> none  [local(): summed = lax.psum(stacked, 'kv')]
    pmax x1 -> x0, blocking collectives: 123 us -> none  [local(): highest = lax.pmax(local_top, 'kv')]
    all_to_all x0 -> x4, blocking collectives: none -> 71 us  [exchange(): lax.all_to_all(jnp.broadcast_to(block[None], (count,) + block.shape), axi...]
    all_to_all x0 -> x2, starting transfers between devices: none -> 19.8 us  [the longest x1 12.4 us: exchange(): lax.all_to_all(jnp.broadcast_to(block[None], (count,) + block.shape), axi...]
    all_to_all x0 -> x2, waiting for transfers between devices: none -> 19 us  [the longest x1 14.3 us: local(): terms = lax.all_to_all(jnp.concatenate([tiles, extra]), KV, 0, 0)]
  transfers between devices with their start and end apart: 1 -> 2, of which waited for: 1 -> 2; matrix products, arithmetic and copies ran while one was open for 0% -> 1% of each run, Pallas kernels for 0% -> 0%
where the time goes in v1:
time: 119 us
  blocking collectives  71 us (60%)
  starting transfers between devices  19.8 us (17%)
  waiting for transfers between devices  19 us (16%)
  other arithmetic  4.75 us (4%)
  matrix products  2.72 us (2%)
    all_to_all x4, blocking collectives, exchange(): lax.all_to_all(jnp.broadcast_to(block[None], (count,) + block.shape), axi...  71 us
    all_to_all x1, waiting for transfers between devices, local(): terms = lax.all_to_all(jnp.concatenate([tiles, extra]), KV, 0, 0)  14.3 us
    all_to_all x1, starting transfers between devices, exchange(): lax.all_to_all(jnp.broadcast_to(block[None], (count,) + block.shape), axi...  12.4 us
    all_to_all x1, starting transfers between devices, local(): terms = lax.all_to_all(jnp.concatenate([tiles, extra]), KV, 0, 0)  7.41 us
    all_to_all x1, waiting for transfers between devices, exchange(): lax.all_to_all(jnp.broadcast_to(block[None], (count,) + block.shape), axi...  4.71 us
  transfers between devices with their start and end apart: 2, of which 2 were waited for; matrix products, arithmetic and copies ran while one was open for 1% of the time, Pallas kernels for 0%

profile of v1, /device:TPU:1, one launch (start us, length us, event | category | flops | bytes accessed | tf_op | source)
XLA Modules:
  0.0 118.7 jit_solution(12186029832131299375)
XLA Ops:
  0.0 0.9 broadcast_compare_fusion
  0.9 1.6 %fusion.48 = (f32[8,8]{1,0:T(8,128)S(1)}, f32[8,8,384]{2,1,0:T(8,128)S(1)}) fusion(bf16[8,8,128]{2,1,0:T(8,128)(2,1)S(1)} %copy-done.5, bf16[8,1,384,128]{3,2,1,0:T(8,128)(2,1)} %param.19, pred[8,384]{1,0:T(8,128)(4,1)S(1)} %broadcast_compare_fusion), kind=kOutput, calls=%fused_computation.99 | convolution fusion | flops 6365120 | bytes 904448 | tf_op jit(solution)/shard_map/sgd,std->sgt/dot_general | solution.py:53
  2.6 0.2 fusion.10
  2.9 0.3 fusion.4
  3.3 30.8 %all_to_all.30 = bf16[16,80,128]{2,1,0:T(8,128)(2,1)S(1)} all-to-all(bf16[16,80,128]{2,1,0:T(8,128)(2,1)S(1)} %broadcast_in_dim.78), channel_id=1, replica_groups=mesh['z'=16,'x'=4,'y'=4,'core'=2] {'z'}, dimensions={0} | all-to-all | bytes 655360 | tf_op jit(solution)/shard_map/all_to_all | solution.py:24
  34.2 0.2 multiply_reduce_fusion
  34.4 8.5 %all_to_all.31 = bf16[4,80,128]{2,1,0:T(8,128)(2,1)S(1)} all-to-all(bf16[4,80,128]{2,1,0:T(8,128)(2,1)S(1)} %broadcast_in_dim.79), channel_id=1, replica_groups=mesh['z'=16,'x'=4,'y'=4,'core'=2] {'x'}, dimensions={0} | all-to-all | bytes 163840 | tf_op jit(solution)/shard_map/all_to_all | solution.py:24
  43.2 0.1 fusion.49
  43.3 0.6 broadcast_in_dim.80
  43.9 12.4 %all-to-all-start.2 = ((f32[8,8,128]{2,1,0:T(8,128)}), f32[8,8,128]{2,1,0:T(8,128)S(1)}, u32[]{:S(2)}, u32[]{:S(2)}) async-start(f32[8,8,128]{2,1,0:T(8,128)} %broadcast_in_dim.80), calls=%async_computation.2 | async-start | bytes 65536 | tf_op jit(solution)/shard_map/all_to_all | solution.py:24
  56.3 4.7 %all-to-all-done.2 = f32[8,8,128]{2,1,0:T(8,128)S(1)} async-done(((f32[8,8,128]{2,1,0:T(8,128)}), f32[8,8,128]{2,1,0:T(8,128)S(1)}, u32[]{:S(2)}, u32[]{:S(2)}) %all-to-all-start.2) | async-done | bytes 32800 | tf_op jit(solution)/shard_map/all_to_all | solution.py:24
  61.1 0.1 multiply_convert_fusion
  61.2 0.2 fusion.1
  61.4 0.2 fusion.2
  61.8 0.6 fusion.8
  62.4 7.4 %all-to-all-start.3 = ((bf16[64,8,128]{2,1,0:T(8,128)(2,1)}), bf16[64,8,128]{2,1,0:T(8,128)(2,1)S(1)}, u32[]{:S(2)}, u32[]{:S(2)}) async-start(bf16[64,8,128]{2,1,0:T(8,128)(2,1)} %fusion.8), calls=%async_computation.3 | async-start | bytes 262144 | tf_op jit(solution)/shard_map/all_to_all | solution.py:86
  69.9 0.6 compare_reduce_fusion
  70.5 14.3 %all-to-all-done.3 = bf16[64,8,128]{2,1,0:T(8,128)(2,1)S(1)} async-done(((bf16[64,8,128]{2,1,0:T(8,128)(2,1)}), bf16[64,8,128]{2,1,0:T(8,128)(2,1)S(1)}, u32[]{:S(2)}, u32[]{:S(2)}) %all-to-all-start.3) | async-done | bytes 131104 | tf_op jit(solution)/shard_map/all_to_all | solution.py:86
  84.9 0.1 slice_reduce_fusion
  85.1 0.7 maximum_select_fusion
  85.9 21.3 %all_to_all.32 = bf16[64,8,128]{2,1,0:T(8,128)(2,1)S(1)} all-to-all(bf16[64,8,128]{2,1,0:T(8,128)(2,1)S(1)} %broadcast_in_dim.81), channel_id=1, replica_groups=mesh['z'=16,'x'=4,'y'=4,'core'=2] {'z','x'}, dimensions={0} | all-to-all | bytes 262144 | tf_op jit(solution)/shard_map/all_to_all | solution.py:24
  107.3 0.2 fusion.12
  107.6 10.5 %all_to_all.33 = f32[8,8,128]{2,1,0:T(8,128)S(1)} all-to-all(f32[8,8,128]{2,1,0:T(8,128)S(1)} %broadcast_in_dim.82), channel_id=1, replica_groups=mesh['z'=16,'x'=4,'y'=4,'core'=2] {'y','core'}, dimensions={0} | all-to-all | bytes 65536 | tf_op jit(solution)/shard_map/all_to_all | solution.py:24
  118.1 0.6 add_convert_fusion
  (57 shorter events, 1.2 us)
Async XLA Ops:
  0.0 61.2 %copy-start = (bf16[128,3584]{1,0:T(8,128)(2,1)S(1)}, bf16[128,3584]{1,0:T(8,128)(2,1)}, u32[]{:S(2)}) copy-start(bf16[128,3584]{1,0:T(8,128)(2,1)} %param.25) | copy-start | bytes 2752516
  0.0 0.9 copy-start.5
  0.0 2.8 %copy-start.3 = (bf16[8,1,384,128]{3,2,1,0:T(8,128)(2,1)S(1)}, bf16[8,1,384,128]{3,2,1,0:T(8,128)(2,1)}, u32[]{:S(2)}) copy-start(bf16[8,1,384,128]{3,2,1,0:T(8,128)(2,1)} %param.20) | copy-start | bytes 2359300
  34.1 22.2 %copy-start.7 = (bf16[128]{0:T(256)(128)(2,1)S(1)}, bf16[128]{0:T(256)(128)(2,1)}, u32[]{:S(2)}) copy-start(bf16[128]{0:T(256)(128)(2,1)} %param.24) | copy-start | bytes 772
  34.2 26.9 %copy-start.6 = (bf16[8,128]{1,0:T(8,128)(2,1)S(1)}, bf16[8,128]{1,0:T(8,128)(2,1)}, u32[]{:S(2)}) copy-start(bf16[8,128]{1,0:T(8,128)(2,1)} %param.22) | copy-start | bytes 6148
  34.4 8.8 %copy-start.4 = (bf16[1024,128]{1,0:T(8,128)(2,1)S(1)}, bf16[1024,128]{1,0:T(8,128)(2,1)}, u32[]{:S(2)}) copy-start(bf16[1024,128]{1,0:T(8,128)(2,1)} %param.23) | copy-start | bytes 786436
  34.4 27.0 %copy-start.1 = (bf16[128,3584]{1,0:T(8,128)(2,1)S(1)}, bf16[128,3584]{1,0:T(8,128)(2,1)}, u32[]{:S(2)}) copy-start(bf16[128,3584]{1,0:T(8,128)(2,1)} %param.26) | copy-start | bytes 2752516
  43.9 17.1 %all-to-all-start.2 = ((f32[8,8,128]{2,1,0:T(8,128)}), f32[8,8,128]{2,1,0:T(8,128)S(1)}, u32[]{:S(2)}, u32[]{:S(2)}) async-start(f32[8,8,128]{2,1,0:T(8,128)} %broadcast_in_dim.80), calls=%async_computation.2 | async-start | bytes 65536 | tf_op jit(solution)/shard_map/all_to_all | solution.py:24
  61.6 45.7 %copy-start.2 = (bf16[3584,128]{1,0:T(8,128)(2,1)S(1)}, bf16[3584,128]{1,0:T(8,128)(2,1)}, u32[]{:S(2)}) copy-start(bf16[3584,128]{1,0:T(8,128)(2,1)} %param.27) | copy-start | bytes 2752516
  62.4 22.4 %all-to-all-start.3 = ((bf16[64,8,128]{2,1,0:T(8,128)(2,1)}), bf16[64,8,128]{2,1,0:T(8,128)(2,1)S(1)}, u32[]{:S(2)}, u32[]{:S(2)}) async-start(bf16[64,8,128]{2,1,0:T(8,128)(2,1)} %fusion.8), calls=%async_computation.3 | async-start | bytes 262144 | tf_op jit(solution)/shard_map/all_to_all | solution.py:86

commit v2 on v1

--- a/solution.py
+++ b/solution.py
@@ -6,9 +6,11 @@
 from jax.sharding import Mesh
 from jax.sharding import PartitionSpec as P
 
-KV = ("z", "x")
+NEAR = ("zl", "x")
+FAR = "zh"
+KV = ("zh", "zl", "x")
 HEAD = ("y", "core")
-NZ, NX, NY, NC = 16, 4, 4, 2
+SIZES = (8, 2, 4, 4, 2)
 NEG = -1e30
 
 
@@ -18,6 +20,10 @@
     middle = lax.reduce_precision(rest, 8, 7)
     low = rest - middle
     return [high.astype(jnp.bfloat16), middle.astype(jnp.bfloat16), low.astype(jnp.bfloat16)]
+
+
+def row_tile(value):
+    return jnp.zeros((8, 128), jnp.bfloat16).at[:, 0:3].set(jnp.stack(pieces(value), axis=1))
 
 
 def exchange(block, axis, count):
@@ -69,37 +75,42 @@
     outs = outs / jnp.where(any_live, total, 1.0)[..., None]
     logs = jnp.where(any_live, top + jnp.log(jnp.where(any_live, total, 1.0)), NEG)
     outs, logs = outs.reshape(64, 128), logs.reshape(64)
-    outs, logs = merge(outs, logs, "z", NZ)
-    outs, logs = merge(outs, logs, "x", NX)
+    outs, logs = merge(outs, logs, NEAR, 8)
+    outs, logs = merge(outs, logs, FAR, 8)
     attended = outs.reshape(batch_rows, 1024).astype(jnp.bfloat16)
     projected = jnp.dot(attended, out_weight, preferred_element_type=jnp.float32)
-    projected = jnp.sum(exchange(projected, HEAD, NY * NC), axis=0)
+    gain = norm_gain.astype(jnp.float32)[None, :]
+    projected, gain = lax.optimization_barrier((projected, gain))
+    projected = jnp.sum(exchange(projected, HEAD, 8), axis=0)
     hidden_state = residual.astype(jnp.float32) + projected
     squares = jnp.sum(hidden_state * hidden_state, axis=1)
-    scaled = (hidden_state * norm_gain.astype(jnp.float32)[None, :]).astype(jnp.bfloat16)
+    scaled = (hidden_state * gain).astype(jnp.bfloat16)
     gate = jnp.dot(scaled, gate_weight, preferred_element_type=jnp.float32)
     up = jnp.dot(scaled, up_weight, preferred_element_type=jnp.float32)
     tiles = jnp.concatenate([gate, up], axis=1).astype(jnp.bfloat16)
-    tiles = tiles.reshape(batch_rows, 56, 128).transpose(1, 0, 2)
-    extra = jnp.zeros((8, 8, 128), jnp.bfloat16)
-    extra = extra.at[0, :, 0:3].set(jnp.stack(pieces(squares), axis=1))
-    terms = lax.all_to_all(jnp.concatenate([tiles, extra]), KV, 0, 0)
+    tiles = tiles.reshape(batch_rows, 8, 7, 128).transpose(1, 2, 0, 3)
+    extra = jnp.broadcast_to(row_tile(squares)[None, None], (8, 1, 8, 128))
+    packed = jnp.concatenate([tiles, extra], axis=1)
+    packed, hidden_state = lax.optimization_barrier((packed, hidden_state))
+    terms = lax.all_to_all(packed, NEAR, 0, 0)
     summed = jnp.sum(terms.astype(jnp.float32), axis=0)
-    special = jnp.zeros((8, 128), jnp.bfloat16)
-    special = special.at[:, 0:3].set(jnp.stack(pieces(jnp.sum(summed[:, 0:3], axis=1)), axis=1))
-    got = exchange(jnp.where(me == 56, special, summed.astype(jnp.bfloat16)), KV, NZ * NX)
-    squares = jnp.sum(got[56, :, 0:3].astype(jnp.float32), axis=1)
+    squares = jnp.sum(summed[7, :, 0:3], axis=1)
+    packed = jnp.concatenate([summed[0:7].astype(jnp.bfloat16), row_tile(squares)[None]])
+    terms = exchange(packed, FAR, 8)
+    summed = jnp.sum(terms.astype(jnp.float32), axis=0)
+    squares = jnp.sum(summed[7, :, 0:3], axis=1)
     scale_row = lax.rsqrt(squares / 8192 + 1e-05)
-    whole = got[0:56].astype(jnp.float32) * scale_row[None, :, None]
+    whole = (summed[0:7] * scale_row[None, :, None]).astype(jnp.bfloat16)
+    whole = exchange(whole, NEAR, 8).reshape(56, 8, 128).astype(jnp.float32)
     activated = (jax.nn.silu(whole[0:28]) * whole[28:56]).astype(jnp.bfloat16)
     activated = activated.transpose(1, 0, 2).reshape(batch_rows, 3584)
     downward = jnp.dot(activated, down_weight, preferred_element_type=jnp.float32)
-    downward = jnp.sum(exchange(downward, HEAD, NY * NC), axis=0)
+    downward = jnp.sum(exchange(downward, HEAD, 8), axis=0)
     return (hidden_state + downward).astype(jnp.bfloat16)
 
 
 def solution(mesh):
-    fine = Mesh(mesh.devices.reshape(NZ, NX, NY, NC), KV + HEAD)
+    fine = Mesh(mesh.devices.reshape(SIZES), KV + HEAD)
     return jax.shard_map(
         local,
         mesh=fine,

time: 119 us -> 106 us (0.89)
  blocking collectives: 71 us -> 55.7 us
  starting transfers between devices: 19.8 us -> 21.6 us
    all_to_all x4, blocking collectives: 71 us -> 47.3 us  [exchange(): lax.all_to_all(jnp.broadcast_to(block[None], (count,) + block.shape), axi...]
    all_to_all x1 -> x0, waiting for transfers between devices: 14.3 us -> none  [local(): terms = lax.all_to_all(jnp.concatenate([tiles, extra]), KV, 0, 0)]
    all_to_all x1 -> x2, waiting for transfers between devices: 4.71 us -> 18.3 us  [exchange(): lax.all_to_all(jnp.broadcast_to(block[None], (count,) + block.shape), axi...]
    all_to_all x1 -> x2, starting transfers between devices: 12.4 us -> 21.6 us  [exchange(): lax.all_to_all(jnp.broadcast_to(block[None], (count,) + block.shape), axi...]
    all_to_all x0 -> x1, blocking collectives: none -> 8.33 us  [local(): terms = lax.all_to_all(packed, NEAR, 0, 0)]
    all_to_all x1 -> x0, starting transfers between devices: 7.41 us -> none  [local(): terms = lax.all_to_all(jnp.concatenate([tiles, extra]), KV, 0, 0)]
    broadcast_in_dim x0 -> x3, other arithmetic: none -> 1.39 us  [the longest x1 0.73 us: local(): row_tile(squares)[None]]
where the time goes in v2:
time: 106 us; the launch traced here: 105 us
  blocking collectives  55.7 us (53%)
  starting transfers between devices  21.6 us (20%)
  waiting for transfers between devices  18.3 us (17%)
  other arithmetic  4.74 us (4%)
  matrix products  2.71 us (3%)
  local copies, waits for them, and re-layouts  1.8 us (2%)
    all_to_all x4, blocking collectives, exchange(): lax.all_to_all(jnp.broadcast_to(block[None], (count,) + block.shape), axi...  47.3 us
    all_to_all x2, starting transfers between devices, exchange(): lax.all_to_all(jnp.broadcast_to(block[None], (count,) + block.shape), axi...  21.6 us
    all_to_all x2, waiting for transfers between devices, exchange(): lax.all_to_all(jnp.broadcast_to(block[None], (count,) + block.shape), axi...  18.3 us
    all_to_all x1, blocking collectives, local(): terms = lax.all_to_all(packed, NEAR, 0, 0)  8.33 us
  transfers between devices with their start and end apart: 2, of which 2 were waited for; matrix products, arithmetic and copies ran while one was open for 1% of the time, Pallas kernels for 0%

profile of v2, /device:TPU:1, one launch (start us, length us, event | category | flops | bytes accessed | tf_op | source)
XLA Modules:
  0.0 105.0 jit_solution(6951514445123730510)
XLA Ops:
  0.0 0.9 broadcast_compare_fusion
  0.9 1.6 %fusion.52 = (f32[8,8]{1,0:T(8,128)S(1)}, f32[8,8,384]{2,1,0:T(8,128)S(1)}) fusion(bf16[8,8,128]{2,1,0:T(8,128)(2,1)S(1)} %copy-done.5, bf16[8,1,384,128]{3,2,1,0:T(8,128)(2,1)} %param.19, pred[8,384]{1,0:T(8,128)(4,1)S(1)} %broadcast_compare_fusion), kind=kOutput, calls=%fused_computation.109 | convolution fusion | flops 6365120 | bytes 904448 | tf_op jit(solution)/shard_map/sgd,std->sgt/dot_general | solution.py:59
  2.6 0.2 fusion.9
  2.9 0.3 fusion.2
  3.2 11.6 %all_to_all.35 = bf16[8,80,128]{2,1,0:T(8,128)(2,1)S(1)} all-to-all(bf16[8,80,128]{2,1,0:T(8,128)(2,1)S(1)} %broadcast_in_dim.98), channel_id=1, replica_groups=mesh['zh'=8,'zl'=2,'x'=4,'y'=4,'core'=2] {'zl','x'}, dimensions={0} | all-to-all | bytes 327680 | tf_op jit(solution)/shard_map/all_to_all | solution.py:30
  15.1 0.7 broadcast_in_dim.99
  15.8 14.1 %all-to-all-start.1 = ((bf16[8,80,128]{2,1,0:T(8,128)(2,1)}), bf16[8,80,128]{2,1,0:T(8,128)(2,1)S(1)}, u32[]{:S(2)}, u32[]{:S(2)}) async-start(bf16[8,80,128]{2,1,0:T(8,128)(2,1)} %broadcast_in_dim.99), calls=%async_computation.1 | async-start | bytes 327680 | tf_op jit(solution)/shard_map/all_to_all | solution.py:30
  29.9 14.2 %all-to-all-done.1 = bf16[8,80,128]{2,1,0:T(8,128)(2,1)S(1)} async-done(((bf16[8,80,128]{2,1,0:T(8,128)(2,1)}), bf16[8,80,128]{2,1,0:T(8,128)(2,1)S(1)}, u32[]{:S(2)}, u32[]{:S(2)}) %all-to-all-start.1) | async-done | bytes 163872 | tf_op jit(solution)/shard_map/all_to_all | solution.py:30
  44.2 0.1 multiply_reduce_fusion
  44.3 0.1 fusion.53
  44.5 0.6 broadcast_in_dim.102
  45.1 7.5 %all-to-all-start.2 = ((f32[8,8,128]{2,1,0:T(8,128)}), f32[8,8,128]{2,1,0:T(8,128)S(1)}, u32[]{:S(2)}, u32[]{:S(2)}) async-start(f32[8,8,128]{2,1,0:T(8,128)} %broadcast_in_dim.102), calls=%async_computation.2 | async-start | bytes 65536 | tf_op jit(solution)/shard_map/all_to_all | solution.py:30
  52.6 0.6 compare_reduce_fusion
  53.3 4.1 %all-to-all-done.2 = f32[8,8,128]{2,1,0:T(8,128)S(1)} async-done(((f32[8,8,128]{2,1,0:T(8,128)}), f32[8,8,128]{2,1,0:T(8,128)S(1)}, u32[]{:S(2)}, u32[]{:S(2)}) %all-to-all-start.2) | async-done | bytes 32800 | tf_op jit(solution)/shard_map/all_to_all | solution.py:30
  57.5 0.7 maximum_select_fusion
  58.2 0.2 convolution_convert_fusion
  58.5 0.2 convolution_convert_fusion.1
  58.8 8.3 %all_to_all.36 = bf16[8,8,8,128]{3,2,1,0:T(8,128)(2,1)S(1)} all-to-all(bf16[8,8,8,128]{3,2,1,0:T(8,128)(2,1)S(1)} %pad_maximum_fusion), channel_id=1, replica_groups=mesh['zh'=8,'zl'=2,'x'=4,'y'=4,'core'=2] {'zl','x'}, dimensions={0} | all-to-all | bytes 262144 | tf_op jit(solution)/shard_map/all_to_all | solution.py:95
  67.3 0.7 maximum_select_fusion.1
  68.1 15.9 %all_to_all.37 = bf16[8,8,8,128]{3,2,1,0:T(8,128)(2,1)S(1)} all-to-all(bf16[8,8,8,128]{3,2,1,0:T(8,128)(2,1)S(1)} %broadcast_in_dim.106), channel_id=1, replica_groups=mesh['zh'=8,'zl'=2,'x'=4,'y'=4,'core'=2] {'zh'}, dimensions={0} | all-to-all | bytes 262144 | tf_op jit(solution)/shard_map/all_to_all | solution.py:30
  84.3 7.7 %all_to_all.38 = bf16[8,7,8,128]{3,2,1,0:T(8,128)(2,1)S(1)} all-to-all(bf16[8,7,8,128]{3,2,1,0:T(8,128)(2,1)S(1)} %broadcast_in_dim.107), channel_id=1, replica_groups=mesh['zh'=8,'zl'=2,'x'=4,'y'=4,'core'=2] {'zl','x'}, dimensions={0} | all-to-all | bytes 229376 | tf_op jit(solution)/shard_map/all_to_all | solution.py:30
  92.1 0.2 fusion.11
  92.4 12.1 %all_to_all.39 = f32[8,8,128]{2,1,0:T(8,128)S(1)} all-to-all(f32[8,8,128]{2,1,0:T(8,128)S(1)} %broadcast_in_dim.108), channel_id=1, replica_groups=mesh['zh'=8,'zl'=2,'x'=4,'y'=4,'core'=2] {'y','core'}, dimensions={0} | all-to-all | bytes 65536 | tf_op jit(solution)/shard_map/all_to_all | solution.py:30
  104.4 0.6 add_convert_fusion
  (65 shorter events, 1.5 us)
Async XLA Ops:
  0.0 58.2 %copy-start = (bf16[128,3584]{1,0:T(8,128)(2,1)S(1)}, bf16[128,3584]{1,0:T(8,128)(2,1)}, u32[]{:S(2)}) copy-start(bf16[128,3584]{1,0:T(8,128)(2,1)} %param.26) | copy-start | bytes 2752516
  0.0 0.9 copy-start.5
  0.0 2.8 %copy-start.3 = (bf16[8,1,384,128]{3,2,1,0:T(8,128)(2,1)S(1)}, bf16[8,1,384,128]{3,2,1,0:T(8,128)(2,1)}, u32[]{:S(2)}) copy-start(bf16[8,1,384,128]{3,2,1,0:T(8,128)(2,1)} %param.20) | copy-start | bytes 2359300
  15.1 14.8 %copy-start.7 = (bf16[128]{0:T(256)(128)(2,1)S(1)}, bf16[128]{0:T(256)(128)(2,1)}, u32[]{:S(2)}) copy-start(bf16[128]{0:T(256)(128)(2,1)} %param.24) | copy-start | bytes 772
  15.1 29.2 %copy-start.4 = (bf16[1024,128]{1,0:T(8,128)(2,1)S(1)}, bf16[1024,128]{1,0:T(8,128)(2,1)}, u32[]{:S(2)}) copy-start(bf16[1024,128]{1,0:T(8,128)(2,1)} %param.23) | copy-start | bytes 786436
  15.1 42.2 %copy-start.6 = (bf16[8,128]{1,0:T(8,128)(2,1)S(1)}, bf16[8,128]{1,0:T(8,128)(2,1)}, u32[]{:S(2)}) copy-start(bf16[8,128]{1,0:T(8,128)(2,1)} %param.22) | copy-start | bytes 6148
  15.8 42.6 %copy-start.1 = (bf16[128,3584]{1,0:T(8,128)(2,1)S(1)}, bf16[128,3584]{1,0:T(8,128)(2,1)}, u32[]{:S(2)}) copy-start(bf16[128,3584]{1,0:T(8,128)(2,1)} %param.25) | copy-start | bytes 2752516
  15.8 28.3 %all-to-all-start.1 = ((bf16[8,80,128]{2,1,0:T(8,128)(2,1)}), bf16[8,80,128]{2,1,0:T(8,128)(2,1)S(1)}, u32[]{:S(2)}, u32[]{:S(2)}) async-start(bf16[8,80,128]{2,1,0:T(8,128)(2,1)} %broadcast_in_dim.99), calls=%async_computation.1 | async-start | bytes 327680 | tf_op jit(solution)/shard_map/all_to_all | solution.py:30
  45.1 12.2 %all-to-all-start.2 = ((f32[8,8,128]{2,1,0:T(8,128)}), f32[8,8,128]{2,1,0:T(8,128)S(1)}, u32[]{:S(2)}, u32[]{:S(2)}) async-start(f32[8,8,128]{2,1,0:T(8,128)} %broadcast_in_dim.102), calls=%async_computation.2 | async-start | bytes 65536 | tf_op jit(solution)/shard_map/all_to_all | solution.py:30
  67.1 25.0 %copy-start.2 = (bf16[3584,128]{1,0:T(8,128)(2,1)S(1)}, bf16[3584,128]{1,0:T(8,128)(2,1)}, u32[]{:S(2)}) copy-start(bf16[3584,128]{1,0:T(8,128)(2,1)} %param.27) | copy-start | bytes 2752516

commit v3 on v2

v3 whole, which is shorter than its diff:
```python
import math

import jax
import jax.numpy as jnp
from jax import lax
from jax.experimental import pallas as pl
from jax.experimental.pallas import tpu as pltpu
from jax.sharding import Mesh
from jax.sharding import PartitionSpec as P

NEAR = ("zl", "x")
FAR = "zh"
KV = ("zh", "zl", "x")
HEAD = ("y", "core")
SIZES = (8, 2, 4, 4, 2)
NEG = -1e30


def pieces(value, masks):
    high = lax.reduce_precision(value, 8, 7)
    middle = lax.reduce_precision(value - high, 8, 7)
    low = value - high - middle
    return (high * masks[0] + middle * masks[1] + low * masks[2]).astype(jnp.bfloat16)


def attend(
    query, keys, values, lengths, gain, packed, row_masks, lane_masks, gain_out,
    q_buf, k_buf, v_buf, l_buf, g_buf, s_sem,
):
    rows, _, block_len, _ = k_buf.shape
    small = [
        pltpu.make_async_copy(lengths, l_buf, s_sem.at[0]),
        pltpu.make_async_copy(query, q_buf, s_sem.at[1]),
        pltpu.make_async_copy(gain, g_buf, s_sem.at[2]),
    ]
    k_in = pltpu.make_async_copy(keys, k_buf, s_sem.at[3])
    v_in = pltpu.make_async_copy(values, v_buf, s_sem.at[4])
    for copy in small + [k_in, v_in]:
        copy.start()
    wide = (16, 128)
    row, lane = lax.broadcasted_iota(jnp.int32, wide, 0), lax.broadcasted_iota(jnp.int32, wide, 1)
    one, zero = jnp.float32(1), jnp.float32(0)
    for i in range(3):
        row_masks[i] = jnp.where(row == i, one, zero)
        lane_masks[i] = jnp.where(lane[0:8] == i, one, zero)
    first = lax.axis_index(KV) * block_len
    place = first + lax.broadcasted_iota(jnp.int32, (8, block_len), 1)
    for copy in small:
        copy.wait()
    gain_out[...] = jnp.broadcast_to(g_buf[...].astype(jnp.float32), (8, 128))
    scores, live = [], []
    k_in.wait()
    for s in range(rows):
        product = lax.dot_general(
            q_buf[s], k_buf[s, 0], (((1,), (1,)), ((), ())), preferred_element_type=jnp.float32
        )
        scores.append(product * (1.0 / math.sqrt(128)))
        live.append(place < l_buf[s])
    tops, totals, expos = [], [], []
    for s in range(rows):
        masked = jnp.where(live[s], scores[s], NEG)
        top = jnp.max(masked, axis=1, keepdims=True)
        expo = jnp.where(live[s], jnp.exp(masked - top), 0.0)
        tops.append(top)
        totals.append(jnp.sum(expo, axis=1, keepdims=True))
        expos.append(expo.astype(jnp.bfloat16))
    outs, logs = [], jnp.zeros((8, 128), jnp.float32)
    sub = row[0:8]
    v_in.wait()
    for s in range(rows):
        some = totals[s] > 0
        total = jnp.where(some, totals[s], 1.0)
        log = jnp.where(some, tops[s] + jnp.log(total), NEG)
        logs = logs + jnp.where(lane[0:8] == sub + 8 * s, jnp.broadcast_to(log, (8, 128)), 0.0)
        out = jnp.dot(expos[s], v_buf[s, 0], preferred_element_type=jnp.float32)
        outs.append(out / total)
    logs = jnp.broadcast_to(jnp.sum(logs, axis=0, keepdims=True), wide)
    high = logs.astype(jnp.bfloat16).astype(jnp.float32)
    middle = (logs - high).astype(jnp.bfloat16).astype(jnp.float32)
    low = logs - high - middle
    tail = jnp.where(row == 0, high, jnp.where(row == 1, middle, jnp.where(row == 2, low, 0.0)))
    block = jnp.concatenate(outs + [tail], axis=0).astype(jnp.bfloat16)
    for d in range(8):
        packed[d] = block


def attention(query, keys, values, lengths, gain):
    f32, bf16 = jnp.float32, jnp.bfloat16
    whole = pl.BlockSpec(memory_space=pltpu.VMEM)
    return pl.pallas_call(
        attend,
        out_shape=(
            pltpu.VMEM((8, 80, 128), bf16),
            pltpu.VMEM((3, 16, 128), f32),
            pltpu.VMEM((3, 8, 128), f32),
            pltpu.VMEM((8, 128), f32),
        ),
        in_specs=[pl.BlockSpec(memory_space=pl.ANY)] * 5,
        out_specs=(whole,) * 4,
        scratch_shapes=[
            pltpu.VMEM(query.shape, bf16),
            pltpu.VMEM(keys.shape, bf16),
            pltpu.VMEM(values.shape, bf16),
            pltpu.SMEM(lengths.shape, jnp.int32),
            pltpu.VMEM((1, 128), bf16),
            pltpu.SemaphoreType.DMA((5,)),
        ],
        compiler_params=pltpu.CompilerParams(vmem_limit_bytes=60 * 2**20),
        name="attention",
    )(query, keys, values, lengths, gain.reshape(1, 128))


def exchange(block, axis, count):
    return lax.all_to_all(jnp.broadcast_to(block[None], (count,) + block.shape), axis, 0, 0)


def merge(got):
    logs = jnp.sum(got[:, 64:80, 0:64].astype(jnp.float32), axis=1)
    top = jnp.max(logs, axis=0)
    share = jnp.exp(logs - top)
    total = jnp.sum(share, axis=0)
    outs = jnp.sum(got[:, 0:64].astype(jnp.float32) * (share / total)[:, :, None], axis=0)
    return outs.astype(jnp.bfloat16), top + jnp.log(total)


def local(
    query,
    key_cache,
    value_cache,
    lengths,
    residual,
    out_weight,
    norm_gain,
    gate_weight,
    up_weight,
    down_weight,
):
    packed, row_masks, lane_masks, gain = attention(
        query, key_cache, value_cache, lengths, norm_gain
    )
    outs, logs = merge(lax.all_to_all(packed, NEAR, 0, 0))
    tail = pieces(jnp.broadcast_to(jnp.concatenate([logs, logs])[None], (16, 128)), row_masks)
    outs, _ = merge(exchange(jnp.concatenate([outs, tail]), FAR, 8))
    attended = outs.reshape(8, 1024)
    projected = jnp.dot(attended, out_weight, preferred_element_type=jnp.float32)
    projected = jnp.sum(exchange(projected, HEAD, 8), axis=0)
    hidden_state = residual.astype(jnp.float32) + projected
    squares = jnp.sum(hidden_state * hidden_state, axis=1, keepdims=True)
    scaled = (hidden_state * gain).astype(jnp.bfloat16)
    gate = jnp.dot(scaled, gate_weight, preferred_element_type=jnp.float32)
    up = jnp.dot(scaled, up_weight, preferred_element_type=jnp.float32)
    tiles = jnp.concatenate([gate, up], axis=1).astype(jnp.bfloat16)
    tiles = tiles.reshape(8, 8, 7, 128).transpose(1, 2, 0, 3)
    extra = jnp.broadcast_to(pieces(jnp.broadcast_to(squares, (8, 128)), lane_masks)[None, None], (8, 1, 8, 128))
    packed = jnp.concatenate([tiles, extra], axis=1)
    packed, hidden_state = lax.optimization_barrier((packed, hidden_state))
    terms = lax.all_to_all(packed, NEAR, 0, 0)
    summed = jnp.sum(terms.astype(jnp.float32), axis=0)
    squares = jnp.sum(summed[7], axis=1, keepdims=True)
    packed = jnp.concatenate([summed[0:7].astype(jnp.bfloat16), pieces(jnp.broadcast_to(squares, (8, 128)), lane_masks)[None]])
    terms = exchange(packed, FAR, 8)
    summed = jnp.sum(terms.astype(jnp.float32), axis=0)
    squares = jnp.sum(summed[7], axis=1, keepdims=True)
    scale_row = lax.rsqrt(squares / 8192 + 1e-05)
    whole = (summed[0:7] * scale_row[None]).astype(jnp.bfloat16)
    whole = exchange(whole, NEAR, 8).reshape(56, 8, 128).astype(jnp.float32)
    activated = (jax.nn.silu(whole[0:28]) * whole[28:56]).astype(jnp.bfloat16)
    activated = activated.transpose(1, 0, 2).reshape(8, 3584)
    downward = jnp.dot(activated, down_weight, preferred_element_type=jnp.float32)
    downward = jnp.sum(exchange(downward, HEAD, 8), axis=0)
    return (hidden_state + downward).astype(jnp.bfloat16)


def solution(mesh):
    fine = Mesh(mesh.devices.reshape(SIZES), KV + HEAD)
    return jax.shard_map(
        local,
        mesh=fine,
        in_specs=(
            P(None, HEAD, None),
            P(None, HEAD, KV, None),
            P(None, HEAD, KV, None),
            P(),
            P(None, KV),
            P(HEAD, KV),
            P(KV),
            P(KV, HEAD),
            P(KV, HEAD),
            P(HEAD, KV),
        ),
        out_specs=P(None, KV),
        check_vma=False,
    )
```

time: 106 us -> 101 us (0.953)
  blocking collectives: 55.7 us -> 95.9 us
  starting transfers between devices: 21.6 us -> 0 us
  waiting for transfers between devices: 18.3 us -> 0 us
  other arithmetic: 4.74 us -> 1.87 us
  Pallas kernels: 0 us -> 2.1 us
  matrix products: 2.71 us -> 0.83 us
  local copies, waits for them, and re-layouts: 1.8 us -> 0.15 us
    all_to_all x4 -> x5, blocking collectives: 47.3 us -> 75.9 us  [exchange(): lax.all_to_all(jnp.broadcast_to(block[None], (count,) + block.shape), axi...]
    all_to_all x2 -> x0, starting transfers between devices: 21.6 us -> none  [exchange(): lax.all_to_all(jnp.broadcast_to(block[None], (count,) + block.shape), axi...]
    all_to_all x2 -> x0, waiting for transfers between devices: 18.3 us -> none  [exchange(): lax.all_to_all(jnp.broadcast_to(block[None], (count,) + block.shape), axi...]
    all_to_all x0 -> x1, blocking collectives: none -> 11.6 us  [local(): outs, logs = merge(lax.all_to_all(packed, NEAR, 0, 0))]
    pallas_call x0 -> x1, Pallas kernels: none -> 2.1 us  [attention(): pl.pallas_call(attend, out_shape=(pltpu.VMEM((8, 80, 128), bf16), pltpu.V...]
    dot_general x2 -> x0, matrix products: 1.88 us -> none  [the longest x1 1.59 us: local(): jnp.einsum('sgd,std->sgt', query, key_cache[:, 0], preferred_element_type...]
    broadcast_in_dim x3 -> x0, other arithmetic: 1.39 us -> none  [the longest x1 0.73 us: local(): row_tile(squares)[None]]
    broadcast_in_dim x6 -> x5, local copies, waits for them, and re-layouts: 1.35 us -> 0.08 us  [exchange(): jnp.broadcast_to(block[None], (count,) + block.shape)]
  transfers between devices with their start and end apart: 2 -> 0, of which waited for: 2 -> 0; matrix products, arithmetic and copies ran while one was open for 1% -> 0% of each run, Pallas kernels for 0% -> 0%
where the time goes in v3:
time: 101 us
  blocking collectives  95.9 us (95%)
  Pallas kernels  2.1 us (2%)
  other arithmetic  1.87 us (2%)
    all_to_all x5, blocking collectives, exchange(): lax.all_to_all(jnp.broadcast_to(block[None], (count,) + block.shape), axi...  75.9 us
    all_to_all x1, blocking collectives, local(): outs, logs = merge(lax.all_to_all(packed, NEAR, 0, 0))  11.6 us
    all_to_all x1, blocking collectives, local(): terms = lax.all_to_all(packed, NEAR, 0, 0)  8.33 us
    pallas_call x1, Pallas kernels, attention(): pl.pallas_call(attend, out_shape=(pltpu.VMEM((8, 80, 128), bf16), pltpu.V...  2.1 us

profile of v3, /device:TPU:1, one launch (start us, length us, event | category | flops | bytes accessed | tf_op | source)
XLA Modules:
  0.0 101.0 jit_solution(10663144685819891354)
XLA Ops:
  0.0 2.1 %attention.1 = (bf16[8,80,128]{2,1,0:T(8,128)(2,1)S(1)}, f32[3,16,128]{2,1,0:T(8,128)S(1)}, f32[3,8,128]{2,1,0:T(8,128)S(1)}, f32[8,128]{1,0:T(8,128)S(1)}) custom-call(bf16[8,8,128]{2,1,0:T(8,128)(2,1)} %query.1, bf16[8,1,384,128]{3,2,1,0:T(8,128)(2,1)} %keys.1, bf16[8,1,384,128]{3,2,1,0:T(8,128)(2,1)} %values.1, s32[8]{0:T(128)} %lengths.1, ...), custom_call_target="tpu_custom_call" | custom-call | tf_op jit(solution)/shard_map/attention/pallas_call | solution.py:90
  2.1 11.6 %all_to_all.35 = bf16[8,80,128]{2,1,0:T(8,128)(2,1)S(1)} all-to-all(bf16[8,80,128]{2,1,0:T(8,128)(2,1)S(1)} %get-tuple-element.11), channel_id=1, replica_groups=mesh['zh'=8,'zl'=2,'x'=4,'y'=4,'core'=2] {'zl','x'}, dimensions={0} | all-to-all | bytes 327680 | tf_op jit(solution)/shard_map/all_to_all | solution.py:141
  13.8 0.1 fusion.17
  13.9 0.1 multiply_reduce_fusion.1
  14.1 0.0 copy-start.3
  14.1 0.0 copy-start.4
  14.1 28.1 %all_to_all.36 = bf16[8,80,128]{2,1,0:T(8,128)(2,1)S(1)} all-to-all(bf16[8,80,128]{2,1,0:T(8,128)(2,1)S(1)} %broadcast_in_dim.33), channel_id=1, replica_groups=mesh['zh'=8,'zl'=2,'x'=4,'y'=4,'core'=2] {'zh'}, dimensions={0} | all-to-all | bytes 327680 | tf_op jit(solution)/shard_map/all_to_all | solution.py:114
  42.3 0.1 multiply_reduce_fusion
  42.5 0.1 fusion.21
  42.6 12.0 %all_to_all.37 = f32[8,8,128]{2,1,0:T(8,128)S(1)} all-to-all(f32[8,8,128]{2,1,0:T(8,128)S(1)} %broadcast_in_dim.34), channel_id=1, replica_groups=mesh['zh'=8,'zl'=2,'x'=4,'y'=4,'core'=2] {'y','core'}, dimensions={0} | all-to-all | bytes 65536 | tf_op jit(solution)/shard_map/all_to_all | solution.py:114
  54.6 0.1 multiply_reduce_fusion.2
  54.8 0.2 convolution_convert_fusion
  55.0 0.2 convolution_convert_fusion.1
  55.3 0.1 fusion.11
  55.4 8.3 %all_to_all.38 = bf16[8,8,8,128]{3,2,1,0:T(8,128)(2,1)S(1)} all-to-all(bf16[8,8,8,128]{3,2,1,0:T(8,128)(2,1)S(1)} %pad_maximum_fusion), channel_id=1, replica_groups=mesh['zh'=8,'zl'=2,'x'=4,'y'=4,'core'=2] {'zl','x'}, dimensions={0} | all-to-all | bytes 262144 | tf_op jit(solution)/shard_map/all_to_all | solution.py:157
  63.7 0.1 slice_reduce_fusion.1
  63.9 0.1 add_convert_fusion.1
  64.0 16.0 %all_to_all.39 = bf16[8,8,8,128]{3,2,1,0:T(8,128)(2,1)S(1)} all-to-all(bf16[8,8,8,128]{3,2,1,0:T(8,128)(2,1)S(1)} %broadcast_in_dim.42), channel_id=1, replica_groups=mesh['zh'=8,'zl'=2,'x'=4,'y'=4,'core'=2] {'zh'}, dimensions={0} | all-to-all | bytes 262144 | tf_op jit(solution)/shard_map/all_to_all | solution.py:114
  80.1 0.1 slice_reduce_fusion
  80.2 0.1 fusion.6
  80.3 7.7 %all_to_all.40 = bf16[8,7,8,128]{3,2,1,0:T(8,128)(2,1)S(1)} all-to-all(bf16[8,7,8,128]{3,2,1,0:T(8,128)(2,1)S(1)} %broadcast_in_dim.43), channel_id=1, replica_groups=mesh['zh'=8,'zl'=2,'x'=4,'y'=4,'core'=2] {'zl','x'}, dimensions={0} | all-to-all | bytes 229376 | tf_op jit(solution)/shard_map/all_to_all | solution.py:114
  88.1 0.2 fusion.4
  88.3 12.1 %all_to_all.41 = f32[8,8,128]{2,1,0:T(8,128)S(1)} all-to-all(f32[8,8,128]{2,1,0:T(8,128)S(1)} %broadcast_in_dim.44), channel_id=1, replica_groups=mesh['zh'=8,'zl'=2,'x'=4,'y'=4,'core'=2] {'y','core'}, dimensions={0} | all-to-all | bytes 65536 | tf_op jit(solution)/shard_map/all_to_all | solution.py:114
  100.4 0.6 add_convert_fusion
  (40 shorter events, 0.5 us)
Async XLA Ops:
  0.0 54.8 %copy-start = (bf16[128,3584]{1,0:T(8,128)(2,1)S(1)}, bf16[128,3584]{1,0:T(8,128)(2,1)}, u32[]{:S(2)}) copy-start(bf16[128,3584]{1,0:T(8,128)(2,1)} %param.18) | copy-start | bytes 2752516
  14.1 28.4 %copy-start.3 = (bf16[1024,128]{1,0:T(8,128)(2,1)S(1)}, bf16[1024,128]{1,0:T(8,128)(2,1)}, u32[]{:S(2)}) copy-start(bf16[1024,128]{1,0:T(8,128)(2,1)} %param.15) | copy-start | bytes 786436
  14.1 40.6 %copy-start.4 = (bf16[8,128]{1,0:T(8,128)(2,1)S(1)}, bf16[8,128]{1,0:T(8,128)(2,1)}, u32[]{:S(2)}) copy-start(bf16[8,128]{1,0:T(8,128)(2,1)} %param.14) | copy-start | bytes 6148
  14.1 40.9 %copy-start.1 = (bf16[128,3584]{1,0:T(8,128)(2,1)S(1)}, bf16[128,3584]{1,0:T(8,128)(2,1)}, u32[]{:S(2)}) copy-start(bf16[128,3584]{1,0:T(8,128)(2,1)} %param.17) | copy-start | bytes 2752516
  63.7 24.4 %copy-start.2 = (bf16[3584,128]{1,0:T(8,128)(2,1)S(1)}, bf16[3584,128]{1,0:T(8,128)(2,1)}, u32[]{:S(2)}) copy-start(bf16[3584,128]{1,0:T(8,128)(2,1)} %param.19) | copy-start | bytes 2752516

commit v4 on v3

--- a/solution.py
+++ b/solution.py
@@ -8,11 +8,11 @@
 from jax.sharding import Mesh
 from jax.sharding import PartitionSpec as P
 
-NEAR = ("zl", "x")
-FAR = "zh"
-KV = ("zh", "zl", "x")
+KV = ("z", "x")
 HEAD = ("y", "core")
-SIZES = (8, 2, 4, 4, 2)
+SIZES = (16, 4, 4, 2)
+FAR = [[2 * pair + (pair // 4 + half) % 2 for pair in range(8)] for half in range(2)]
+NEAR = [[FAR[half][pair] * 4 + x for half in range(2) for x in range(4)] for pair in range(8)]
 NEG = -1e30
 
 
@@ -37,12 +37,12 @@
     v_in = pltpu.make_async_copy(values, v_buf, s_sem.at[4])
     for copy in small + [k_in, v_in]:
         copy.start()
-    wide = (16, 128)
+    wide = (8, 128)
     row, lane = lax.broadcasted_iota(jnp.int32, wide, 0), lax.broadcasted_iota(jnp.int32, wide, 1)
     one, zero = jnp.float32(1), jnp.float32(0)
     for i in range(3):
         row_masks[i] = jnp.where(row == i, one, zero)
-        lane_masks[i] = jnp.where(lane[0:8] == i, one, zero)
+        lane_masks[i] = jnp.where(lane == i, one, zero)
     first = lax.axis_index(KV) * block_len
     place = first + lax.broadcasted_iota(jnp.int32, (8, block_len), 1)
     for copy in small:
@@ -65,13 +65,12 @@
         totals.append(jnp.sum(expo, axis=1, keepdims=True))
         expos.append(expo.astype(jnp.bfloat16))
     outs, logs = [], jnp.zeros((8, 128), jnp.float32)
-    sub = row[0:8]
     v_in.wait()
     for s in range(rows):
         some = totals[s] > 0
         total = jnp.where(some, totals[s], 1.0)
         log = jnp.where(some, tops[s] + jnp.log(total), NEG)
-        logs = logs + jnp.where(lane[0:8] == sub + 8 * s, jnp.broadcast_to(log, (8, 128)), 0.0)
+        logs = logs + jnp.where(lane == row + 8 * s, jnp.broadcast_to(log, (8, 128)), 0.0)
         out = jnp.dot(expos[s], v_buf[s, 0], preferred_element_type=jnp.float32)
         outs.append(out / total)
     logs = jnp.broadcast_to(jnp.sum(logs, axis=0, keepdims=True), wide)
@@ -90,8 +89,8 @@
     return pl.pallas_call(
         attend,
         out_shape=(
-            pltpu.VMEM((8, 80, 128), bf16),
-            pltpu.VMEM((3, 16, 128), f32),
+            pltpu.VMEM((8, 72, 128), bf16),
+            pltpu.VMEM((3, 8, 128), f32),
             pltpu.VMEM((3, 8, 128), f32),
             pltpu.VMEM((8, 128), f32),
         ),
@@ -110,12 +109,24 @@
     )(query, keys, values, lengths, gain.reshape(1, 128))
 
 
-def exchange(block, axis, count):
-    return lax.all_to_all(jnp.broadcast_to(block[None], (count,) + block.shape), axis, 0, 0)
+def near(blocks):
+    return lax.all_to_all(blocks, KV, 0, 0, axis_index_groups=NEAR)
+
+
+def far(blocks):
+    return lax.all_to_all(blocks, "z", 0, 0, axis_index_groups=FAR)
+
+
+def heads(blocks):
+    return lax.all_to_all(blocks, HEAD, 0, 0)
+
+
+def spread(block):
+    return jnp.broadcast_to(block[None], (8,) + block.shape)
 
 
 def merge(got):
-    logs = jnp.sum(got[:, 64:80, 0:64].astype(jnp.float32), axis=1)
+    logs = jnp.sum(got[:, 64:72, 0:64].astype(jnp.float32), axis=1)
     top = jnp.max(logs, axis=0)
     share = jnp.exp(logs - top)
     total = jnp.sum(share, axis=0)
@@ -138,12 +149,12 @@
     packed, row_masks, lane_masks, gain = attention(
         query, key_cache, value_cache, lengths, norm_gain
     )
-    outs, logs = merge(lax.all_to_all(packed, NEAR, 0, 0))
-    tail = pieces(jnp.broadcast_to(jnp.concatenate([logs, logs])[None], (16, 128)), row_masks)
-    outs, _ = merge(exchange(jnp.concatenate([outs, tail]), FAR, 8))
+    outs, logs = merge(near(packed))
+    tail = pieces(jnp.broadcast_to(jnp.concatenate([logs, logs])[None], (8, 128)), row_masks)
+    outs, _ = merge(far(spread(jnp.concatenate([outs, tail]))))
     attended = outs.reshape(8, 1024)
     projected = jnp.dot(attended, out_weight, preferred_element_type=jnp.float32)
-    projected = jnp.sum(exchange(projected, HEAD, 8), axis=0)
+    projected = jnp.sum(heads(spread(projected)), axis=0)
     hidden_state = residual.astype(jnp.float32) + projected
     squares = jnp.sum(hidden_state * hidden_state, axis=1, keepdims=True)
     scaled = (hidden_state * gain).astype(jnp.bfloat16)
@@ -154,20 +165,20 @@
     extra = jnp.broadcast_to(pieces(jnp.broadcast_to(squares, (8, 128)), lane_masks)[None, None], (8, 1, 8, 128))
     packed = jnp.concatenate([tiles, extra], axis=1)
     packed, hidden_state = lax.optimization_barrier((packed, hidden_state))
-    terms = lax.all_to_all(packed, NEAR, 0, 0)
+    terms = near(packed)
     summed = jnp.sum(terms.astype(jnp.float32), axis=0)
     squares = jnp.sum(summed[7], axis=1, keepdims=True)
     packed = jnp.concatenate([summed[0:7].astype(jnp.bfloat16), pieces(jnp.broadcast_to(squares, (8, 128)), lane_masks)[None]])
-    terms = exchange(packed, FAR, 8)
+    terms = far(spread(packed))
     summed = jnp.sum(terms.astype(jnp.float32), axis=0)
     squares = jnp.sum(summed[7], axis=1, keepdims=True)
     scale_row = lax.rsqrt(squares / 8192 + 1e-05)
     whole = (summed[0:7] * scale_row[None]).astype(jnp.bfloat16)
-    whole = exchange(whole, NEAR, 8).reshape(56, 8, 128).astype(jnp.float32)
+    whole = near(spread(whole)).reshape(56, 8, 128).astype(jnp.float32)
     activated = (jax.nn.silu(whole[0:28]) * whole[28:56]).astype(jnp.bfloat16)
     activated = activated.transpose(1, 0, 2).reshape(8, 3584)
     downward = jnp.dot(activated, down_weight, preferred_element_type=jnp.float32)
-    downward = jnp.sum(exchange(downward, HEAD, 8), axis=0)
+    downward = jnp.sum(heads(spread(downward)), axis=0)
     return (hidden_state + downward).astype(jnp.bfloat16)
 
 

time: 101 us -> 100 us (0.990)
  blocking collectives: 95.9 us -> 94.7 us
    all_to_all x7, blocking collectives: 95.9 us -> 94.7 us  [the longest x2 43.4 us: far(): return lax.all_to_all(blocks, 'z', 0, 0, axis_index_groups=FAR)]
where the time goes in v4:
time: 100 us; the launch traced here: 99.8 us
  blocking collectives  94.7 us (95%)
  Pallas kernels  2.1 us (2%)
  other arithmetic  1.86 us (2%)
    all_to_all x2, blocking collectives, far(): return lax.all_to_all(blocks, 'z', 0, 0, axis_index_groups=FAR)  43.4 us
    all_to_all x3, blocking collectives, near(): return lax.all_to_all(blocks, KV, 0, 0, axis_index_groups=NEAR)  27.2 us
    all_to_all x2, blocking collectives, heads(): return lax.all_to_all(blocks, HEAD, 0, 0)  24.1 us
    pallas_call x1, Pallas kernels, attention(): pl.pallas_call(attend, out_shape=(pltpu.VMEM((8, 72, 128), bf16), pltpu.V...  2.1 us

profile of v4, /device:TPU:1, one launch (start us, length us, event | category | flops | bytes accessed | tf_op | source)
XLA Modules:
  0.0 99.8 jit_solution(8129806285885612328)
XLA Ops:
  0.0 2.1 %attention.1 = (bf16[8,72,128]{2,1,0:T(8,128)(2,1)S(1)}, f32[3,8,128]{2,1,0:T(8,128)S(1)}, f32[3,8,128]{2,1,0:T(8,128)S(1)}, f32[8,128]{1,0:T(8,128)S(1)}) custom-call(bf16[8,8,128]{2,1,0:T(8,128)(2,1)} %query.1, bf16[8,1,384,128]{3,2,1,0:T(8,128)(2,1)} %keys.1, bf16[8,1,384,128]{3,2,1,0:T(8,128)(2,1)} %values.1, s32[8]{0:T(128)} %lengths.1, ...), custom_call_target="tpu_custom_call" | custom-call | tf_op jit(solution)/shard_map/attention/pallas_call | solution.py:89
  2.1 11.5 %all_to_all.35 = bf16[8,72,128]{2,1,0:T(8,128)(2,1)S(1)} all-to-all(bf16[8,72,128]{2,1,0:T(8,128)(2,1)S(1)} %get-tuple-element.11), channel_id=1, replica_groups={{0,8,16,24,32,40,48,56},{64,72,80,88,96,104,112,120},{128,136,144,152,1..., dimensions={0} | all-to-all | bytes 294912 | tf_op jit(solution)/shard_map/all_to_all | solution.py:113
  13.7 0.1 fusion.17
  13.8 0.1 multiply_reduce_fusion.1
  14.0 0.0 copy-start.3
  14.0 27.5 %all_to_all.36 = bf16[8,72,128]{2,1,0:T(8,128)(2,1)S(1)} all-to-all(bf16[8,72,128]{2,1,0:T(8,128)(2,1)S(1)} %broadcast_in_dim.33), channel_id=1, replica_groups={{0,64,128,192,288,352,416,480},{32,96,160,224,256,320,384,448},{1,65,12..., dimensions={0} | all-to-all | bytes 294912 | tf_op jit(solution)/shard_map/all_to_all | solution.py:117
  41.6 0.1 multiply_reduce_fusion
  41.8 0.1 fusion.21
  41.9 12.1 %all_to_all.37 = f32[8,8,128]{2,1,0:T(8,128)S(1)} all-to-all(f32[8,8,128]{2,1,0:T(8,128)S(1)} %broadcast_in_dim.34), channel_id=1, replica_groups=mesh['z'=16,'x'=4,'y'=4,'core'=2] {'y','core'}, dimensions={0} | all-to-all | bytes 65536 | tf_op jit(solution)/shard_map/all_to_all | solution.py:121
  54.1 0.1 multiply_reduce_fusion.2
  54.2 0.2 convolution_convert_fusion
  54.4 0.2 convolution_convert_fusion.1
  54.7 0.1 fusion.8
  54.8 7.9 %all_to_all.38 = bf16[8,8,8,128]{3,2,1,0:T(8,128)(2,1)S(1)} all-to-all(bf16[8,8,8,128]{3,2,1,0:T(8,128)(2,1)S(1)} %pad_maximum_fusion), channel_id=1, replica_groups={{0,8,16,24,32,40,48,56},{64,72,80,88,96,104,112,120},{128,136,144,152,1..., dimensions={0} | all-to-all | bytes 262144 | tf_op jit(solution)/shard_map/all_to_all | solution.py:113
  62.8 0.0 copy-start.2
  62.8 0.1 slice_reduce_fusion.1
  62.9 0.1 add_convert_fusion.1
  63.0 15.9 %all_to_all.39 = bf16[8,8,8,128]{3,2,1,0:T(8,128)(2,1)S(1)} all-to-all(bf16[8,8,8,128]{3,2,1,0:T(8,128)(2,1)S(1)} %broadcast_in_dim.42), channel_id=1, replica_groups={{0,64,128,192,288,352,416,480},{32,96,160,224,256,320,384,448},{1,65,12..., dimensions={0} | all-to-all | bytes 262144 | tf_op jit(solution)/shard_map/all_to_all | solution.py:117
  78.9 0.1 slice_reduce_fusion
  79.1 0.1 fusion.6
  79.2 7.7 %all_to_all.40 = bf16[8,7,8,128]{3,2,1,0:T(8,128)(2,1)S(1)} all-to-all(bf16[8,7,8,128]{3,2,1,0:T(8,128)(2,1)S(1)} %broadcast_in_dim.43), channel_id=1, replica_groups={{0,8,16,24,32,40,48,56},{64,72,80,88,96,104,112,120},{128,136,144,152,1..., dimensions={0} | all-to-all | bytes 229376 | tf_op jit(solution)/shard_map/all_to_all | solution.py:113
  87.0 0.2 fusion.4
  87.2 12.0 %all_to_all.41 = f32[8,8,128]{2,1,0:T(8,128)S(1)} all-to-all(f32[8,8,128]{2,1,0:T(8,128)S(1)} %broadcast_in_dim.44), channel_id=1, replica_groups=mesh['z'=16,'x'=4,'y'=4,'core'=2] {'y','core'}, dimensions={0} | all-to-all | bytes 65536 | tf_op jit(solution)/shard_map/all_to_all | solution.py:121
  99.2 0.6 add_convert_fusion
  (40 shorter events, 0.5 us)
Async XLA Ops:
  0.0 54.2 %copy-start = (bf16[128,3584]{1,0:T(8,128)(2,1)S(1)}, bf16[128,3584]{1,0:T(8,128)(2,1)}, u32[]{:S(2)}) copy-start(bf16[128,3584]{1,0:T(8,128)(2,1)} %param.18) | copy-start | bytes 2752516
  14.0 27.8 %copy-start.3 = (bf16[1024,128]{1,0:T(8,128)(2,1)S(1)}, bf16[1024,128]{1,0:T(8,128)(2,1)}, u32[]{:S(2)}) copy-start(bf16[1024,128]{1,0:T(8,128)(2,1)} %param.15) | copy-start | bytes 786436
  14.0 40.1 %copy-start.4 = (bf16[8,128]{1,0:T(8,128)(2,1)S(1)}, bf16[8,128]{1,0:T(8,128)(2,1)}, u32[]{:S(2)}) copy-start(bf16[8,128]{1,0:T(8,128)(2,1)} %param.14) | copy-start | bytes 6148
  14.0 40.4 %copy-start.1 = (bf16[128,3584]{1,0:T(8,128)(2,1)S(1)}, bf16[128,3584]{1,0:T(8,128)(2,1)}, u32[]{:S(2)}) copy-start(bf16[128,3584]{1,0:T(8,128)(2,1)} %param.17) | copy-start | bytes 2752516
  62.8 24.2 %copy-start.2 = (bf16[3584,128]{1,0:T(8,128)(2,1)S(1)}, bf16[3584,128]{1,0:T(8,128)(2,1)}, u32[]{:S(2)}) copy-start(bf16[3584,128]{1,0:T(8,128)(2,1)} %param.19) | copy-start | bytes 2752516

commit v5 on v4

v5 whole, which is shorter than its diff:
```python
import math

import jax
import jax.numpy as jnp
from jax import lax
from jax.experimental import pallas as pl
from jax.experimental.pallas import tpu as pltpu
from jax.sharding import Mesh
from jax.sharding import PartitionSpec as P

KV = ("z", "x")
HEAD = ("y", "core")
SIZES = (16, 4, 4, 2)
FAR = [[2 * pair + (pair // 4 + half) % 2 for pair in range(8)] for half in range(2)]
NEAR = [[FAR[half][pair] * 4 + x for half in range(2) for x in range(4)] for pair in range(8)]
NEG = -1e30


def attend(
    query, keys, values, lengths, gain, packed, gain_out,
    q_buf, k_buf, v_buf, l_buf, g_buf, s_sem,
):
    rows, _, block_len, _ = k_buf.shape
    small = [
        pltpu.make_async_copy(lengths, l_buf, s_sem.at[0]),
        pltpu.make_async_copy(query, q_buf, s_sem.at[1]),
        pltpu.make_async_copy(gain, g_buf, s_sem.at[2]),
    ]
    k_in = pltpu.make_async_copy(keys, k_buf, s_sem.at[3])
    v_in = pltpu.make_async_copy(values, v_buf, s_sem.at[4])
    for copy in small + [k_in, v_in]:
        copy.start()
    wide = (8, 128)
    row, lane = lax.broadcasted_iota(jnp.int32, wide, 0), lax.broadcasted_iota(jnp.int32, wide, 1)
    first = lax.axis_index(KV) * block_len
    place = first + lax.broadcasted_iota(jnp.int32, (8, block_len), 1)
    for copy in small:
        copy.wait()
    gain_out[...] = jnp.broadcast_to(g_buf[...].astype(jnp.float32), (8, 128))
    scores, live = [], []
    k_in.wait()
    for s in range(rows):
        product = lax.dot_general(
            q_buf[s], k_buf[s, 0], (((1,), (1,)), ((), ())), preferred_element_type=jnp.float32
        )
        scores.append(product * (1.0 / math.sqrt(128)))
        live.append(place < l_buf[s])
    tops, totals, expos = [], [], []
    for s in range(rows):
        masked = jnp.where(live[s], scores[s], NEG)
        top = jnp.max(masked, axis=1, keepdims=True)
        expo = jnp.where(live[s], jnp.exp(masked - top), 0.0)
        tops.append(top)
        totals.append(jnp.sum(expo, axis=1, keepdims=True))
        expos.append(expo.astype(jnp.bfloat16))
    outs, logs = [], jnp.zeros((8, 128), jnp.float32)
    v_in.wait()
    for s in range(rows):
        some = totals[s] > 0
        total = jnp.where(some, totals[s], 1.0)
        log = jnp.where(some, tops[s] + jnp.log(total), NEG)
        logs = logs + jnp.where(lane == row + 8 * s, jnp.broadcast_to(log, (8, 128)), 0.0)
        out = jnp.dot(expos[s], v_buf[s, 0], preferred_element_type=jnp.float32)
        outs.append(out / total)
    tail = tail_of(jnp.sum(logs, axis=0, keepdims=True))
    block = jnp.concatenate(outs + [tail], axis=0).astype(jnp.bfloat16)
    for d in range(8):
        packed[d] = block


def attention(query, keys, values, lengths, gain):
    f32, bf16 = jnp.float32, jnp.bfloat16
    whole = pl.BlockSpec(memory_space=pltpu.VMEM)
    return pl.pallas_call(
        attend,
        out_shape=(
            pltpu.VMEM((8, 72, 128), bf16),
            pltpu.VMEM((8, 128), f32),
        ),
        in_specs=[pl.BlockSpec(memory_space=pl.ANY)] * 5,
        out_specs=(whole,) * 2,
        scratch_shapes=[
            pltpu.VMEM(query.shape, bf16),
            pltpu.VMEM(keys.shape, bf16),
            pltpu.VMEM(values.shape, bf16),
            pltpu.SMEM(lengths.shape, jnp.int32),
            pltpu.VMEM((1, 128), bf16),
            pltpu.SemaphoreType.DMA((5,)),
        ],
        compiler_params=pltpu.CompilerParams(vmem_limit_bytes=60 * 2**20),
        name="attention",
    )(query, keys, values, lengths, gain.reshape(1, 128))


def near(blocks):
    return lax.all_to_all(blocks, KV, 0, 0, axis_index_groups=NEAR)


def far(blocks):
    return lax.all_to_all(blocks, "z", 0, 0, axis_index_groups=FAR)


def heads(blocks):
    return lax.all_to_all(blocks, HEAD, 0, 0)


def spread(block):
    return jnp.broadcast_to(block[None], (8,) + block.shape)


def tail_of(logs):
    row = lax.broadcasted_iota(jnp.int32, (8, 128), 0)
    logs = jnp.broadcast_to(logs, (8, 128))
    high = logs.astype(jnp.bfloat16).astype(jnp.float32)
    middle = (logs - high).astype(jnp.bfloat16).astype(jnp.float32)
    low = logs - high - middle
    return jnp.where(row == 0, high, jnp.where(row == 1, middle, jnp.where(row == 2, low, 0.0)))


def merged(got):
    parts = [got[i].astype(jnp.float32) for i in range(8)]
    logs = jnp.concatenate([jnp.sum(p[64:72], axis=0, keepdims=True) for p in parts], axis=0)
    top = jnp.max(logs, axis=0, keepdims=True)
    share = jnp.exp(logs - top)
    total = jnp.sum(share, axis=0, keepdims=True)
    weights = jnp.transpose(share / total)
    outs = parts[0][0:64] * weights[0:64, 0:1]
    for i in range(1, 8):
        outs = outs + parts[i][0:64] * weights[0:64, i : i + 1]
    return outs, top + jnp.log(total)


def merge_near(got, packed):
    outs, logs = merged(got)
    block = jnp.concatenate([outs, tail_of(logs)], axis=0).astype(jnp.bfloat16)
    for i in range(8):
        packed[i] = block


def merge_far(got, out):
    out[...] = merged(got)[0].astype(jnp.bfloat16)


def summed(terms):
    total = terms[0].astype(jnp.float32)
    for i in range(1, 8):
        total = total + terms[i].astype(jnp.float32)
    return total, jnp.sum(total[7], axis=1, keepdims=True)


def row_tile(value):
    lane = lax.broadcasted_iota(jnp.int32, (8, 128), 1)
    value = jnp.broadcast_to(value, (8, 128))
    high = value.astype(jnp.bfloat16).astype(jnp.float32)
    middle = (value - high).astype(jnp.bfloat16).astype(jnp.float32)
    low = value - high - middle
    return jnp.where(lane == 0, high, jnp.where(lane == 1, middle, jnp.where(lane == 2, low, 0.0)))


def gate_up(terms, residual, gain, gate_weight, up_weight, hidden_out, packed):
    hidden = residual[...].astype(jnp.float32)
    projected = terms[0]
    for i in range(1, 8):
        projected = projected + terms[i]
    hidden = hidden + projected
    hidden_out[...] = hidden
    scaled = (hidden * gain[...]).astype(jnp.bfloat16)
    tile = row_tile(jnp.sum(hidden * hidden, axis=1, keepdims=True)).astype(jnp.bfloat16)
    for i in range(8):
        packed[i, 7] = tile
    for first, weight in ((0, gate_weight), (28, up_weight)):
        product = jnp.dot(scaled, weight[...], preferred_element_type=jnp.float32)
        for t in range(28):
            place = first + t
            packed[place // 7, place % 7] = product[:, 128 * t : 128 * t + 128].astype(jnp.bfloat16)


def sum_near(terms, packed):
    total, squares = summed(terms)
    block = jnp.concatenate([total[0:7], row_tile(squares)[None]], axis=0).astype(jnp.bfloat16)
    for i in range(8):
        packed[i] = block


def sum_far(terms, packed):
    total, squares = summed(terms)
    block = (total[0:7] * lax.rsqrt(squares / 8192 + 1e-05)[None]).astype(jnp.bfloat16)
    for i in range(8):
        packed[i] = block


def step(body, shapes, count=1):
    whole = pl.BlockSpec(memory_space=pltpu.VMEM)
    return pl.pallas_call(
        body,
        out_shape=tuple(pltpu.VMEM(shape, dtype) for shape, dtype in shapes),
        in_specs=[whole] * count,
        out_specs=(whole,) * len(shapes),
        compiler_params=pltpu.CompilerParams(vmem_limit_bytes=4 * 2**20),
        name=body.__name__,
    )


def local(
    query,
    key_cache,
    value_cache,
    lengths,
    residual,
    out_weight,
    norm_gain,
    gate_weight,
    up_weight,
    down_weight,
):
    f32, bf16 = jnp.float32, jnp.bfloat16
    packed, gain = attention(query, key_cache, value_cache, lengths, norm_gain)
    (packed,) = step(merge_near, [((8, 72, 128), bf16)])(near(packed))
    (outs,) = step(merge_far, [((64, 128), bf16)])(far(packed))
    attended = outs.reshape(8, 1024)
    projected = jnp.dot(attended, out_weight, preferred_element_type=f32)
    hidden_state, packed = step(gate_up, [((8, 128), f32), ((8, 8, 8, 128), bf16)], 5)(
        heads(spread(projected)), residual, gain, gate_weight, up_weight
    )
    (packed,) = step(sum_near, [((8, 8, 8, 128), bf16)])(near(packed))
    (packed,) = step(sum_far, [((8, 7, 8, 128), bf16)])(far(packed))
    whole = near(packed).reshape(56, 8, 128).astype(jnp.float32)
    activated = (jax.nn.silu(whole[0:28]) * whole[28:56]).astype(jnp.bfloat16)
    activated = activated.transpose(1, 0, 2).reshape(8, 3584)
    downward = jnp.dot(activated, down_weight, preferred_element_type=jnp.float32)
    downward = jnp.sum(heads(spread(downward)), axis=0)
    return (hidden_state + downward).astype(jnp.bfloat16)


def solution(mesh):
    fine = Mesh(mesh.devices.reshape(SIZES), KV + HEAD)
    return jax.shard_map(
        local,
        mesh=fine,
        in_specs=(
            P(None, HEAD, None),
            P(None, HEAD, KV, None),
            P(None, HEAD, KV, None),
            P(),
            P(None, KV),
            P(HEAD, KV),
            P(KV),
            P(KV, HEAD),
            P(KV, HEAD),
            P(HEAD, KV),
        ),
        out_specs=P(None, KV),
        check_vma=False,
    )
```

time: 100 us -> 99.5 us (level)
  other arithmetic: 1.86 us -> 0.64 us
  Pallas kernels: 2.1 us -> 3.28 us
    pallas_call x0 -> x5, Pallas kernels: none -> 1.11 us  [the longest x1 0.34 us: local(): step(gate_up, [((8, 128), f32), ((8, 8, 8, 128), bf16)], 5)]
where the time goes in v5:
time: 99.5 us; the launch traced here: 99.1 us
  blocking collectives  94.7 us (95%)
  Pallas kernels  3.28 us (3%)
    all_to_all x2, blocking collectives, far(): return lax.all_to_all(blocks, 'z', 0, 0, axis_index_groups=FAR)  43.1 us
    all_to_all x3, blocking collectives, near(): return lax.all_to_all(blocks, KV, 0, 0, axis_index_groups=NEAR)  27.3 us
    all_to_all x2, blocking collectives, heads(): return lax.all_to_all(blocks, HEAD, 0, 0)  24.2 us
    pallas_call x1, Pallas kernels, attention(): pl.pallas_call(attend, out_shape=(pltpu.VMEM((8, 72, 128), bf16), pltpu.V...  2.17 us

profile of v5, /device:TPU:1, one launch (start us, length us, event | category | flops | bytes accessed | tf_op | source)
XLA Modules:
  0.0 99.1 jit_solution(7172077062508675955)
XLA Ops:
  0.0 0.0 copy-start
  0.0 0.0 copy-start.4
  0.0 2.2 %attention.1 = (bf16[8,72,128]{2,1,0:T(8,128)(2,1)S(1)}, f32[8,128]{1,0:T(8,128)S(1)}) custom-call(bf16[8,8,128]{2,1,0:T(8,128)(2,1)} %query.1, bf16[8,1,384,128]{3,2,1,0:T(8,128)(2,1)} %keys.1, bf16[8,1,384,128]{3,2,1,0:T(8,128)(2,1)} %values.1, s32[8]{0:T(128)} %lengths.1, bf16[1,128]{1,0:T(2,128)(2,1)} %bitcast.26), custom_call_target="tpu_custom_call" | custom-call | tf_op jit(solution)/shard_map/attention/pallas_call | solution.py:74
  2.2 0.0 copy-start.1
  2.2 11.7 %all_to_all.35.got = bf16[8,72,128]{2,1,0:T(8,128)(2,1)S(1)} all-to-all(bf16[8,72,128]{2,1,0:T(8,128)(2,1)S(1)} %get-tuple-element.9), channel_id=1, replica_groups={{0,8,16,24,32,40,48,56},{64,72,80,88,96,104,112,120},{128,136,144,152,1..., dimensions={0} | all-to-all | bytes 294912 | tf_op jit(solution)/shard_map/all_to_all | solution.py:96
  13.8 0.3 merge_near.1
  14.1 27.4 %all_to_all.36.got = bf16[8,72,128]{2,1,0:T(8,128)(2,1)S(1)} all-to-all(bf16[8,72,128]{2,1,0:T(8,128)(2,1)S(1)} %merge_near.1), channel_id=1, replica_groups={{0,64,128,192,288,352,416,480},{32,96,160,224,256,320,384,448},{1,65,12..., dimensions={0} | all-to-all | bytes 294912 | tf_op jit(solution)/shard_map/all_to_all | solution.py:100
  41.5 0.3 merge_far.1
  41.8 0.0 copy-done.4
  41.8 0.1 fusion.7
  42.0 12.3 %all_to_all.37.terms = f32[8,8,128]{2,1,0:T(8,128)S(1)} all-to-all(f32[8,8,128]{2,1,0:T(8,128)S(1)} %broadcast_in_dim.4), channel_id=1, replica_groups=mesh['z'=16,'x'=4,'y'=4,'core'=2] {'y','core'}, dimensions={0} | all-to-all | bytes 65536 | tf_op jit(solution)/shard_map/all_to_all | solution.py:104
  54.3 0.0 copy-done.2
  54.3 0.0 copy-done.1
  54.3 0.0 copy-done.3
  54.3 0.3 gate_up.1
  54.6 7.9 %all_to_all.38.terms = bf16[8,8,8,128]{3,2,1,0:T(8,128)(2,1)S(1)} all-to-all(bf16[8,8,8,128]{3,2,1,0:T(8,128)(2,1)S(1)} %get-tuple-element.12), channel_id=1, replica_groups={{0,8,16,24,32,40,48,56},{64,72,80,88,96,104,112,120},{128,136,144,152,1..., dimensions={0} | all-to-all | bytes 262144 | tf_op jit(solution)/shard_map/all_to_all | solution.py:96
  62.6 0.1 sum_near.1
  62.6 15.7 %all_to_all.39.terms = bf16[8,8,8,128]{3,2,1,0:T(8,128)(2,1)S(1)} all-to-all(bf16[8,8,8,128]{3,2,1,0:T(8,128)(2,1)S(1)} %sum_near.1), channel_id=1, replica_groups={{0,64,128,192,288,352,416,480},{32,96,160,224,256,320,384,448},{1,65,12..., dimensions={0} | all-to-all | bytes 262144 | tf_op jit(solution)/shard_map/all_to_all | solution.py:100
  78.4 0.1 sum_far.1
  78.5 7.7 %all_to_all.40 = bf16[8,7,8,128]{3,2,1,0:T(8,128)(2,1)S(1)} all-to-all(bf16[8,7,8,128]{3,2,1,0:T(8,128)(2,1)S(1)} %sum_far.1), channel_id=1, replica_groups={{0,8,16,24,32,40,48,56},{64,72,80,88,96,104,112,120},{128,136,144,152,1..., dimensions={0} | all-to-all | bytes 229376 | tf_op jit(solution)/shard_map/all_to_all | solution.py:96
  86.3 0.0 copy-done
  86.3 0.2 fusion.4
  86.5 12.0 %all_to_all.41 = f32[8,8,128]{2,1,0:T(8,128)S(1)} all-to-all(f32[8,8,128]{2,1,0:T(8,128)S(1)} %broadcast_in_dim.5), channel_id=1, replica_groups=mesh['z'=16,'x'=4,'y'=4,'core'=2] {'y','core'}, dimensions={0} | all-to-all | bytes 65536 | tf_op jit(solution)/shard_map/all_to_all | solution.py:104
  98.5 0.6 add_convert_fusion
  (8 shorter events, 0.1 us)
Async XLA Ops:
  0.0 86.3 %copy-start = (bf16[3584,128]{1,0:T(8,128)(2,1)S(1)}, bf16[3584,128]{1,0:T(8,128)(2,1)}, u32[]{:S(2)}) copy-start(bf16[3584,128]{1,0:T(8,128)(2,1)} %param.19) | copy-start | bytes 2752516
  0.0 41.8 %copy-start.4 = (bf16[1024,128]{1,0:T(8,128)(2,1)S(1)}, bf16[1024,128]{1,0:T(8,128)(2,1)}, u32[]{:S(2)}) copy-start(bf16[1024,128]{1,0:T(8,128)(2,1)} %param.15) | copy-start | bytes 786436
  0.0 54.3 %copy-start.2 = (bf16[128,3584]{1,0:T(8,128)(2,1)S(1)}, bf16[128,3584]{1,0:T(8,128)(2,1)}, u32[]{:S(2)}) copy-start(bf16[128,3584]{1,0:T(8,128)(2,1)} %up_weight.1) | copy-start | bytes 2752516
  2.2 52.1 %copy-start.1 = (bf16[128,3584]{1,0:T(8,128)(2,1)S(1)}, bf16[128,3584]{1,0:T(8,128)(2,1)}, u32[]{:S(2)}) copy-start(bf16[128,3584]{1,0:T(8,128)(2,1)} %gate_weight.1) | copy-start | bytes 2752516
  42.0 12.3 %copy-start.3 = (bf16[8,128]{1,0:T(8,128)(2,1)S(1)}, bf16[8,128]{1,0:T(8,128)(2,1)}, u32[]{:S(2)}) copy-start(bf16[8,128]{1,0:T(8,128)(2,1)} %residual.1) | copy-start | bytes 6148

commit v6 on v5

--- a/solution.py
+++ b/solution.py
@@ -13,6 +13,7 @@
 SIZES = (16, 4, 4, 2)
 FAR = [[2 * pair + (pair // 4 + half) % 2 for pair in range(8)] for half in range(2)]
 NEAR = [[FAR[half][pair] * 4 + x for half in range(2) for x in range(4)] for pair in range(8)]
+FAR = [[members[pair] for pair in (4, 3, 5, 2, 6, 1, 7, 0)] for members in FAR]
 NEG = -1e30
 
 
@@ -28,7 +29,7 @@
     ]
     k_in = pltpu.make_async_copy(keys, k_buf, s_sem.at[3])
     v_in = pltpu.make_async_copy(values, v_buf, s_sem.at[4])
-    for copy in small + [k_in, v_in]:
+    for copy in small[0:2] + [k_in, v_in, small[2]]:
         copy.start()
     wide = (8, 128)
     row, lane = lax.broadcasted_iota(jnp.int32, wide, 0), lax.broadcasted_iota(jnp.int32, wide, 1)
@@ -104,10 +105,6 @@
     return lax.all_to_all(blocks, HEAD, 0, 0)
 
 
-def spread(block):
-    return jnp.broadcast_to(block[None], (8,) + block.shape)
-
-
 def tail_of(logs):
     row = lax.broadcasted_iota(jnp.int32, (8, 128), 0)
     logs = jnp.broadcast_to(logs, (8, 128))
@@ -137,8 +134,13 @@
         packed[i] = block
 
 
-def merge_far(got, out):
-    out[...] = merged(got)[0].astype(jnp.bfloat16)
+def project(got, weight, terms, rows):
+    rows[...] = merged(got)[0]
+    attended = [rows[pl.ds(head, 8, stride=8), :] for head in range(8)]
+    attended = jnp.concatenate(attended, axis=1).astype(jnp.bfloat16)
+    product = jnp.dot(attended, weight[...], preferred_element_type=jnp.float32)
+    for i in range(8):
+        terms[i] = product
 
 
 def summed(terms):
@@ -189,13 +191,26 @@
         packed[i] = block
 
 
-def step(body, shapes, count=1):
+def feed_down(got, weight, terms):
+    tiles = []
+    for t in range(28):
+        gate = got[t // 7, t % 7].astype(jnp.float32)
+        up = got[4 + t // 7, t % 7].astype(jnp.float32)
+        tiles.append((gate / (1.0 + jnp.exp(-gate)) * up).astype(jnp.bfloat16))
+    activated = jnp.concatenate(tiles, axis=1)
+    product = jnp.dot(activated, weight[...], preferred_element_type=jnp.float32)
+    for i in range(8):
+        terms[i] = product
+
+
+def step(body, shapes, count=1, scratch=()):
     whole = pl.BlockSpec(memory_space=pltpu.VMEM)
     return pl.pallas_call(
         body,
         out_shape=tuple(pltpu.VMEM(shape, dtype) for shape, dtype in shapes),
         in_specs=[whole] * count,
         out_specs=(whole,) * len(shapes),
+        scratch_shapes=scratch,
         compiler_params=pltpu.CompilerParams(vmem_limit_bytes=4 * 2**20),
         name=body.__name__,
     )
@@ -216,20 +231,16 @@
     f32, bf16 = jnp.float32, jnp.bfloat16
     packed, gain = attention(query, key_cache, value_cache, lengths, norm_gain)
     (packed,) = step(merge_near, [((8, 72, 128), bf16)])(near(packed))
-    (outs,) = step(merge_far, [((64, 128), bf16)])(far(packed))
-    attended = outs.reshape(8, 1024)
-    projected = jnp.dot(attended, out_weight, preferred_element_type=f32)
+    rows = pltpu.VMEM((64, 128), f32)
+    (terms,) = step(project, [((8, 8, 128), f32)], 2, [rows])(far(packed), out_weight)
     hidden_state, packed = step(gate_up, [((8, 128), f32), ((8, 8, 8, 128), bf16)], 5)(
-        heads(spread(projected)), residual, gain, gate_weight, up_weight
+        heads(terms), residual, gain, gate_weight, up_weight
     )
     (packed,) = step(sum_near, [((8, 8, 8, 128), bf16)])(near(packed))
     (packed,) = step(sum_far, [((8, 7, 8, 128), bf16)])(far(packed))
-    whole = near(packed).reshape(56, 8, 128).astype(jnp.float32)
-    activated = (jax.nn.silu(whole[0:28]) * whole[28:56]).astype(jnp.bfloat16)
-    activated = activated.transpose(1, 0, 2).reshape(8, 3584)
-    downward = jnp.dot(activated, down_weight, preferred_element_type=jnp.float32)
-    downward = jnp.sum(heads(spread(downward)), axis=0)
-    return (hidden_state + downward).astype(jnp.bfloat16)
+    (terms,) = step(feed_down, [((8, 8, 128), f32)], 2)(near(packed), down_weight)
+    downward = jnp.sum(heads(terms), axis=0)
+    return (hidden_state + downward).astype(bf16)
 
 
 def solution(mesh):

time: 99.5 us -> 92.7 us (0.932)
  blocking collectives: 94.7 us -> 88.1 us
    all_to_all x2, blocking collectives: 24.2 us -> 20.8 us  [heads(): return lax.all_to_all(blocks, HEAD, 0, 0)]
    all_to_all x2, blocking collectives: 43.1 us -> 39.9 us  [far(): return lax.all_to_all(blocks, 'z', 0, 0, axis_index_groups=FAR)]
where the time goes in v6:
time: 92.7 us; the launch traced here: 92.3 us
  blocking collectives  88.1 us (95%)
  Pallas kernels  3.58 us (4%)
    all_to_all x2, blocking collectives, far(): return lax.all_to_all(blocks, 'z', 0, 0, axis_index_groups=FAR)  39.9 us
    all_to_all x3, blocking collectives, near(): return lax.all_to_all(blocks, KV, 0, 0, axis_index_groups=NEAR)  27.4 us
    all_to_all x2, blocking collectives, heads(): return lax.all_to_all(blocks, HEAD, 0, 0)  20.8 us
    pallas_call x1, Pallas kernels, attention(): pl.pallas_call(attend, out_shape=(pltpu.VMEM((8, 72, 128), bf16), pltpu.V...  2.1 us

profile of v6, /device:TPU:1, one launch (start us, length us, event | category | flops | bytes accessed | tf_op | source)
XLA Modules:
  0.0 92.3 jit_solution(13242934295235007010)
XLA Ops:
  0.0 0.0 copy-start.3
  0.0 0.0 copy-start.1
  0.0 2.1 %attention.1 = (bf16[8,72,128]{2,1,0:T(8,128)(2,1)S(1)}, f32[8,128]{1,0:T(8,128)S(1)}) custom-call(bf16[8,8,128]{2,1,0:T(8,128)(2,1)} %query.1, bf16[8,1,384,128]{3,2,1,0:T(8,128)(2,1)} %keys.1, bf16[8,1,384,128]{3,2,1,0:T(8,128)(2,1)} %values.1, s32[8]{0:T(128)} %lengths.1, bf16[1,128]{1,0:T(2,128)(2,1)} %bitcast.1), custom_call_target="tpu_custom_call" | custom-call | tf_op jit(solution)/shard_map/attention/pallas_call | solution.py:75
  2.1 0.0 copy-start
  2.1 11.7 %all_to_all.35.got = bf16[8,72,128]{2,1,0:T(8,128)(2,1)S(1)} all-to-all(bf16[8,72,128]{2,1,0:T(8,128)(2,1)S(1)} %get-tuple-element.9), channel_id=1, replica_groups={{0,8,16,24,32,40,48,56},{64,72,80,88,96,104,112,120},{128,136,144,152,1..., dimensions={0} | all-to-all | bytes 294912 | tf_op jit(solution)/shard_map/all_to_all | solution.py:97
  13.8 0.3 merge_near.1
  14.1 22.9 %all_to_all.36.got = bf16[8,72,128]{2,1,0:T(8,128)(2,1)S(1)} all-to-all(bf16[8,72,128]{2,1,0:T(8,128)(2,1)S(1)} %merge_near.1), channel_id=1, replica_groups={{288,192,352,128,416,64,480,0},{256,224,320,160,384,96,448,32},{289,193..., dimensions={0} | all-to-all | bytes 294912 | tf_op jit(solution)/shard_map/all_to_all | solution.py:101
  37.0 0.0 copy-done.3
  37.0 0.4 project.1
  37.4 0.0 copy-start.4
  37.4 11.0 %all_to_all.37.terms = f32[8,8,128]{2,1,0:T(8,128)S(1)} all-to-all(f32[8,8,128]{2,1,0:T(8,128)S(1)} %project.1), channel_id=1, replica_groups=mesh['z'=16,'x'=4,'y'=4,'core'=2] {'y','core'}, dimensions={0} | all-to-all | bytes 65536 | tf_op jit(solution)/shard_map/all_to_all | solution.py:105
  48.4 0.0 copy-done.1
  48.4 0.0 copy-done
  48.4 0.0 copy-done.4
  48.4 0.3 gate_up.1
  48.8 8.1 %all_to_all.38.terms = bf16[8,8,8,128]{3,2,1,0:T(8,128)(2,1)S(1)} all-to-all(bf16[8,8,8,128]{3,2,1,0:T(8,128)(2,1)S(1)} %get-tuple-element.12), channel_id=1, replica_groups={{0,8,16,24,32,40,48,56},{64,72,80,88,96,104,112,120},{128,136,144,152,1..., dimensions={0} | all-to-all | bytes 262144 | tf_op jit(solution)/shard_map/all_to_all | solution.py:97
  56.8 0.1 sum_near.1
  56.9 16.9 %all_to_all.39.terms = bf16[8,8,8,128]{3,2,1,0:T(8,128)(2,1)S(1)} all-to-all(bf16[8,8,8,128]{3,2,1,0:T(8,128)(2,1)S(1)} %sum_near.1), channel_id=1, replica_groups={{288,192,352,128,416,64,480,0},{256,224,320,160,384,96,448,32},{289,193..., dimensions={0} | all-to-all | bytes 262144 | tf_op jit(solution)/shard_map/all_to_all | solution.py:101
  73.9 0.1 sum_far.1
  74.0 7.7 %all_to_all.40.got = bf16[8,7,8,128]{3,2,1,0:T(8,128)(2,1)S(1)} all-to-all(bf16[8,7,8,128]{3,2,1,0:T(8,128)(2,1)S(1)} %sum_far.1), channel_id=1, replica_groups={{0,8,16,24,32,40,48,56},{64,72,80,88,96,104,112,120},{128,136,144,152,1..., dimensions={0} | all-to-all | bytes 229376 | tf_op jit(solution)/shard_map/all_to_all | solution.py:97
  81.7 0.0 copy-done.2
  81.7 0.2 feed_down.1
  81.9 9.8 %all_to_all.41 = f32[8,8,128]{2,1,0:T(8,128)S(1)} all-to-all(f32[8,8,128]{2,1,0:T(8,128)S(1)} %feed_down.1), channel_id=1, replica_groups=mesh['z'=16,'x'=4,'y'=4,'core'=2] {'y','core'}, dimensions={0} | all-to-all | bytes 65536 | tf_op jit(solution)/shard_map/all_to_all | solution.py:105
  91.7 0.6 add_convert_fusion
  (2 shorter events, 0.0 us)
Async XLA Ops:
  0.0 37.0 %copy-start.3 = (bf16[1024,128]{1,0:T(8,128)(2,1)S(1)}, bf16[1024,128]{1,0:T(8,128)(2,1)}, u32[]{:S(2)}) copy-start(bf16[1024,128]{1,0:T(8,128)(2,1)} %weight.2) | copy-start | bytes 786436
  0.0 48.4 %copy-start.1 = (bf16[128,3584]{1,0:T(8,128)(2,1)S(1)}, bf16[128,3584]{1,0:T(8,128)(2,1)}, u32[]{:S(2)}) copy-start(bf16[128,3584]{1,0:T(8,128)(2,1)} %up_weight.1) | copy-start | bytes 2752516
  2.1 46.3 %copy-start = (bf16[128,3584]{1,0:T(8,128)(2,1)S(1)}, bf16[128,3584]{1,0:T(8,128)(2,1)}, u32[]{:S(2)}) copy-start(bf16[128,3584]{1,0:T(8,128)(2,1)} %gate_weight.1) | copy-start | bytes 2752516
  37.4 11.0 %copy-start.4 = (bf16[8,128]{1,0:T(8,128)(2,1)S(1)}, bf16[8,128]{1,0:T(8,128)(2,1)}, u32[]{:S(2)}) copy-start(bf16[8,128]{1,0:T(8,128)(2,1)} %residual.1) | copy-start | bytes 6148
  48.7 33.0 %copy-start.2 = (bf16[3584,128]{1,0:T(8,128)(2,1)S(1)}, bf16[3584,128]{1,0:T(8,128)(2,1)}, u32[]{:S(2)}) copy-start(bf16[3584,128]{1,0:T(8,128)(2,1)} %weight.3) | copy-start | bytes 2752516

commit v7 on v6

--- a/solution.py
+++ b/solution.py
@@ -11,9 +11,9 @@
 KV = ("z", "x")
 HEAD = ("y", "core")
 SIZES = (16, 4, 4, 2)
-FAR = [[2 * pair + (pair // 4 + half) % 2 for pair in range(8)] for half in range(2)]
-NEAR = [[FAR[half][pair] * 4 + x for half in range(2) for x in range(4)] for pair in range(8)]
-FAR = [[members[pair] for pair in (4, 3, 5, 2, 6, 1, 7, 0)] for members in FAR]
+FAR = [[2 * k + (k // 4 + half) % 2 for k in (4, 0, 5, 3, 6, 2, 7, 1)] for half in range(2)]
+NEAR = [[FAR[half][k] * 4 + x for half in (1, 0) for x in (2, 0, 1, 3)] for k in range(8)]
+HEADS = [[5, 7, 3, 1, 4, 6, 2, 0]]
 NEG = -1e30
 
 
@@ -102,7 +102,7 @@
 
 
 def heads(blocks):
-    return lax.all_to_all(blocks, HEAD, 0, 0)
+    return lax.all_to_all(blocks, HEAD, 0, 0, axis_index_groups=HEADS)
 
 
 def tail_of(logs):

time: 92.7 us -> 89.7 us (0.968)
  blocking collectives: 88.1 us -> 85 us
    all_to_all x3, blocking collectives: 27.4 us -> 24.7 us  [near(): return lax.all_to_all(blocks, KV, 0, 0, axis_index_groups=NEAR)]
    all_to_all x2, blocking collectives: 20.8 us -> 19.2 us  [heads(): return lax.all_to_all(blocks, HEAD, 0, 0, axis_index_groups=HEADS)]
    all_to_all x2, blocking collectives: 39.9 us -> 41.1 us  [far(): return lax.all_to_all(blocks, 'z', 0, 0, axis_index_groups=FAR)]
where the time goes in v7:
time: 89.7 us; the launch traced here: 89.3 us
  blocking collectives  85 us (95%)
  Pallas kernels  3.58 us (4%)
    all_to_all x2, blocking collectives, far(): return lax.all_to_all(blocks, 'z', 0, 0, axis_index_groups=FAR)  41.1 us
    all_to_all x3, blocking collectives, near(): return lax.all_to_all(blocks, KV, 0, 0, axis_index_groups=NEAR)  24.7 us
    all_to_all x2, blocking collectives, heads(): return lax.all_to_all(blocks, HEAD, 0, 0, axis_index_groups=HEADS)  19.2 us
    pallas_call x1, Pallas kernels, attention(): pl.pallas_call(attend, out_shape=(pltpu.VMEM((8, 72, 128), bf16), pltpu.V...  2.1 us

profile of v7, /device:TPU:1, one launch (start us, length us, event | category | flops | bytes accessed | tf_op | source)
XLA Modules:
  0.0 89.3 jit_solution(14703472537706239184)
XLA Ops:
  0.0 0.0 copy-start.3
  0.0 0.0 copy-start.1
  0.0 2.1 %attention.1 = (bf16[8,72,128]{2,1,0:T(8,128)(2,1)S(1)}, f32[8,128]{1,0:T(8,128)S(1)}) custom-call(bf16[8,8,128]{2,1,0:T(8,128)(2,1)} %query.1, bf16[8,1,384,128]{3,2,1,0:T(8,128)(2,1)} %keys.1, bf16[8,1,384,128]{3,2,1,0:T(8,128)(2,1)} %values.1, s32[8]{0:T(128)} %lengths.1, bf16[1,128]{1,0:T(2,128)(2,1)} %bitcast.1), custom_call_target="tpu_custom_call" | custom-call | tf_op jit(solution)/shard_map/attention/pallas_call | solution.py:75
  2.1 0.0 copy-start
  2.1 9.7 %all_to_all.35.got = bf16[8,72,128]{2,1,0:T(8,128)(2,1)S(1)} all-to-all(bf16[8,72,128]{2,1,0:T(8,128)(2,1)S(1)} %get-tuple-element.9), channel_id=1, replica_groups={{272,256,264,280,304,288,296,312},{48,32,40,56,16,0,8,24},{336,320,328,..., dimensions={0} | all-to-all | bytes 294912 | tf_op jit(solution)/shard_map/all_to_all | solution.py:97
  11.8 0.3 merge_near.1
  12.1 23.7 %all_to_all.36.got = bf16[8,72,128]{2,1,0:T(8,128)(2,1)S(1)} all-to-all(bf16[8,72,128]{2,1,0:T(8,128)(2,1)S(1)} %merge_near.1), channel_id=1, replica_groups={{288,0,352,192,416,128,480,64},{256,32,320,224,384,160,448,96},{289,1,3..., dimensions={0} | all-to-all | bytes 294912 | tf_op jit(solution)/shard_map/all_to_all | solution.py:101
  35.8 0.0 copy-done.3
  35.8 0.4 project.1
  36.3 0.0 copy-start.4
  36.3 9.3 %all_to_all.37.terms = f32[8,8,128]{2,1,0:T(8,128)S(1)} all-to-all(f32[8,8,128]{2,1,0:T(8,128)S(1)} %project.1), channel_id=1, replica_groups={{5,7,3,1,4,6,2,0},{13,15,11,9,12,14,10,8},{21,23,19,17,20,22,18,16},{29..., dimensions={0} | all-to-all | bytes 65536 | tf_op jit(solution)/shard_map/all_to_all | solution.py:105
  45.5 0.0 copy-done.1
  45.5 0.0 copy-done
  45.5 0.0 copy-done.4
  45.5 0.3 gate_up.1
  45.9 7.8 %all_to_all.38.terms = bf16[8,8,8,128]{3,2,1,0:T(8,128)(2,1)S(1)} all-to-all(bf16[8,8,8,128]{3,2,1,0:T(8,128)(2,1)S(1)} %get-tuple-element.12), channel_id=1, replica_groups={{272,256,264,280,304,288,296,312},{48,32,40,56,16,0,8,24},{336,320,328,..., dimensions={0} | all-to-all | bytes 262144 | tf_op jit(solution)/shard_map/all_to_all | solution.py:97
  53.6 0.1 sum_near.1
  53.7 17.4 %all_to_all.39.terms = bf16[8,8,8,128]{3,2,1,0:T(8,128)(2,1)S(1)} all-to-all(bf16[8,8,8,128]{3,2,1,0:T(8,128)(2,1)S(1)} %sum_near.1), channel_id=1, replica_groups={{288,0,352,192,416,128,480,64},{256,32,320,224,384,160,448,96},{289,1,3..., dimensions={0} | all-to-all | bytes 262144 | tf_op jit(solution)/shard_map/all_to_all | solution.py:101
  71.2 0.1 sum_far.1
  71.3 7.2 %all_to_all.40.got = bf16[8,7,8,128]{3,2,1,0:T(8,128)(2,1)S(1)} all-to-all(bf16[8,7,8,128]{3,2,1,0:T(8,128)(2,1)S(1)} %sum_far.1), channel_id=1, replica_groups={{272,256,264,280,304,288,296,312},{48,32,40,56,16,0,8,24},{336,320,328,..., dimensions={0} | all-to-all | bytes 229376 | tf_op jit(solution)/shard_map/all_to_all | solution.py:97
  78.5 0.0 copy-done.2
  78.5 0.2 feed_down.1
  78.7 10.0 %all_to_all.41 = f32[8,8,128]{2,1,0:T(8,128)S(1)} all-to-all(f32[8,8,128]{2,1,0:T(8,128)S(1)} %feed_down.1), channel_id=1, replica_groups={{5,7,3,1,4,6,2,0},{13,15,11,9,12,14,10,8},{21,23,19,17,20,22,18,16},{29..., dimensions={0} | all-to-all | bytes 65536 | tf_op jit(solution)/shard_map/all_to_all | solution.py:105
  88.7 0.6 add_convert_fusion
  (2 shorter events, 0.0 us)
Async XLA Ops:
  0.0 35.8 %copy-start.3 = (bf16[1024,128]{1,0:T(8,128)(2,1)S(1)}, bf16[1024,128]{1,0:T(8,128)(2,1)}, u32[]{:S(2)}) copy-start(bf16[1024,128]{1,0:T(8,128)(2,1)} %weight.2) | copy-start | bytes 786436
  0.0 45.5 %copy-start.1 = (bf16[128,3584]{1,0:T(8,128)(2,1)S(1)}, bf16[128,3584]{1,0:T(8,128)(2,1)}, u32[]{:S(2)}) copy-start(bf16[128,3584]{1,0:T(8,128)(2,1)} %up_weight.1) | copy-start | bytes 2752516
  2.1 43.4 %copy-start = (bf16[128,3584]{1,0:T(8,128)(2,1)S(1)}, bf16[128,3584]{1,0:T(8,128)(2,1)}, u32[]{:S(2)}) copy-start(bf16[128,3584]{1,0:T(8,128)(2,1)} %gate_weight.1) | copy-start | bytes 2752516
  36.3 9.3 %copy-start.4 = (bf16[8,128]{1,0:T(8,128)(2,1)S(1)}, bf16[8,128]{1,0:T(8,128)(2,1)}, u32[]{:S(2)}) copy-start(bf16[8,128]{1,0:T(8,128)(2,1)} %residual.1) | copy-start | bytes 6148
  45.9 32.6 %copy-start.2 = (bf16[3584,128]{1,0:T(8,128)(2,1)S(1)}, bf16[3584,128]{1,0:T(8,128)(2,1)}, u32[]{:S(2)}) copy-start(bf16[3584,128]{1,0:T(8,128)(2,1)} %weight.3) | copy-start | bytes 2752516

commit v8 on v7

--- a/solution.py
+++ b/solution.py
@@ -12,7 +12,7 @@
 HEAD = ("y", "core")
 SIZES = (16, 4, 4, 2)
 FAR = [[2 * k + (k // 4 + half) % 2 for k in (4, 0, 5, 3, 6, 2, 7, 1)] for half in range(2)]
-NEAR = [[FAR[half][k] * 4 + x for half in (1, 0) for x in (2, 0, 1, 3)] for k in range(8)]
+NEAR = [[FAR[half][k] * 4 + x for half in (0, 1) for x in (2, 0, 1, 3)] for k in range(8)]
 HEADS = [[5, 7, 3, 1, 4, 6, 2, 0]]
 NEG = -1e30
 

time: 89.7 us -> 89.1 us (level)
    all_to_all x2, blocking collectives: 41.1 us -> 39.3 us  [far(): return lax.all_to_all(blocks, 'z', 0, 0, axis_index_groups=FAR)]
    all_to_all x3, blocking collectives: 24.7 us -> 25.9 us  [near(): return lax.all_to_all(blocks, KV, 0, 0, axis_index_groups=NEAR)]
where the time goes in v8:
time: 89.1 us; the launch traced here: 88.8 us
  blocking collectives  84.5 us (95%)
  Pallas kernels  3.58 us (4%)
    all_to_all x2, blocking collectives, far(): return lax.all_to_all(blocks, 'z', 0, 0, axis_index_groups=FAR)  39.3 us
    all_to_all x3, blocking collectives, near(): return lax.all_to_all(blocks, KV, 0, 0, axis_index_groups=NEAR)  25.9 us
    all_to_all x2, blocking collectives, heads(): return lax.all_to_all(blocks, HEAD, 0, 0, axis_index_groups=HEADS)  19.4 us
    pallas_call x1, Pallas kernels, attention(): pl.pallas_call(attend, out_shape=(pltpu.VMEM((8, 72, 128), bf16), pltpu.V...  2.1 us

profile of v8, /device:TPU:1, one launch (start us, length us, event | category | flops | bytes accessed | tf_op | source)
XLA Modules:
  0.0 88.8 jit_solution(17451426314718718304)
XLA Ops:
  0.0 0.0 copy-start.3
  0.0 0.0 copy-start.1
  0.0 2.1 %attention.1 = (bf16[8,72,128]{2,1,0:T(8,128)(2,1)S(1)}, f32[8,128]{1,0:T(8,128)S(1)}) custom-call(bf16[8,8,128]{2,1,0:T(8,128)(2,1)} %query.1, bf16[8,1,384,128]{3,2,1,0:T(8,128)(2,1)} %keys.1, bf16[8,1,384,128]{3,2,1,0:T(8,128)(2,1)} %values.1, s32[8]{0:T(128)} %lengths.1, bf16[1,128]{1,0:T(2,128)(2,1)} %bitcast.1), custom_call_target="tpu_custom_call" | custom-call | tf_op jit(solution)/shard_map/attention/pallas_call | solution.py:75
  2.1 0.0 copy-start
  2.1 10.2 %all_to_all.35.got = bf16[8,72,128]{2,1,0:T(8,128)(2,1)S(1)} all-to-all(bf16[8,72,128]{2,1,0:T(8,128)(2,1)S(1)} %get-tuple-element.9), channel_id=1, replica_groups={{304,288,296,312,272,256,264,280},{16,0,8,24,48,32,40,56},{368,352,360,..., dimensions={0} | all-to-all | bytes 294912 | tf_op jit(solution)/shard_map/all_to_all | solution.py:97
  12.3 0.3 merge_near.1
  12.6 22.9 %all_to_all.36.got = bf16[8,72,128]{2,1,0:T(8,128)(2,1)S(1)} all-to-all(bf16[8,72,128]{2,1,0:T(8,128)(2,1)S(1)} %merge_near.1), channel_id=1, replica_groups={{288,0,352,192,416,128,480,64},{256,32,320,224,384,160,448,96},{289,1,3..., dimensions={0} | all-to-all | bytes 294912 | tf_op jit(solution)/shard_map/all_to_all | solution.py:101
  35.5 0.0 copy-done.3
  35.5 0.4 project.1
  35.9 0.0 copy-start.4
  35.9 9.4 %all_to_all.37.terms = f32[8,8,128]{2,1,0:T(8,128)S(1)} all-to-all(f32[8,8,128]{2,1,0:T(8,128)S(1)} %project.1), channel_id=1, replica_groups={{5,7,3,1,4,6,2,0},{13,15,11,9,12,14,10,8},{21,23,19,17,20,22,18,16},{29..., dimensions={0} | all-to-all | bytes 65536 | tf_op jit(solution)/shard_map/all_to_all | solution.py:105
  45.3 0.0 copy-done.1
  45.3 0.0 copy-done
  45.3 0.0 copy-done.4
  45.3 0.3 gate_up.1
  45.6 8.0 %all_to_all.38.terms = bf16[8,8,8,128]{3,2,1,0:T(8,128)(2,1)S(1)} all-to-all(bf16[8,8,8,128]{3,2,1,0:T(8,128)(2,1)S(1)} %get-tuple-element.12), channel_id=1, replica_groups={{304,288,296,312,272,256,264,280},{16,0,8,24,48,32,40,56},{368,352,360,..., dimensions={0} | all-to-all | bytes 262144 | tf_op jit(solution)/shard_map/all_to_all | solution.py:97
  53.7 0.1 sum_near.1
  53.7 16.4 %all_to_all.39.terms = bf16[8,8,8,128]{3,2,1,0:T(8,128)(2,1)S(1)} all-to-all(bf16[8,8,8,128]{3,2,1,0:T(8,128)(2,1)S(1)} %sum_near.1), channel_id=1, replica_groups={{288,0,352,192,416,128,480,64},{256,32,320,224,384,160,448,96},{289,1,3..., dimensions={0} | all-to-all | bytes 262144 | tf_op jit(solution)/shard_map/all_to_all | solution.py:101
  70.2 0.1 sum_far.1
  70.3 7.6 %all_to_all.40.got = bf16[8,7,8,128]{3,2,1,0:T(8,128)(2,1)S(1)} all-to-all(bf16[8,7,8,128]{3,2,1,0:T(8,128)(2,1)S(1)} %sum_far.1), channel_id=1, replica_groups={{304,288,296,312,272,256,264,280},{16,0,8,24,48,32,40,56},{368,352,360,..., dimensions={0} | all-to-all | bytes 229376 | tf_op jit(solution)/shard_map/all_to_all | solution.py:97
  77.9 0.0 copy-done.2
  77.9 0.2 feed_down.1
  78.1 10.0 %all_to_all.41 = f32[8,8,128]{2,1,0:T(8,128)S(1)} all-to-all(f32[8,8,128]{2,1,0:T(8,128)S(1)} %feed_down.1), channel_id=1, replica_groups={{5,7,3,1,4,6,2,0},{13,15,11,9,12,14,10,8},{21,23,19,17,20,22,18,16},{29..., dimensions={0} | all-to-all | bytes 65536 | tf_op jit(solution)/shard_map/all_to_all | solution.py:105
  88.2 0.6 add_convert_fusion
  (2 shorter events, 0.0 us)
Async XLA Ops:
  0.0 35.5 %copy-start.3 = (bf16[1024,128]{1,0:T(8,128)(2,1)S(1)}, bf16[1024,128]{1,0:T(8,128)(2,1)}, u32[]{:S(2)}) copy-start(bf16[1024,128]{1,0:T(8,128)(2,1)} %weight.2) | copy-start | bytes 786436
  0.0 45.3 %copy-start.1 = (bf16[128,3584]{1,0:T(8,128)(2,1)S(1)}, bf16[128,3584]{1,0:T(8,128)(2,1)}, u32[]{:S(2)}) copy-start(bf16[128,3584]{1,0:T(8,128)(2,1)} %up_weight.1) | copy-start | bytes 2752516
  2.1 43.1 %copy-start = (bf16[128,3584]{1,0:T(8,128)(2,1)S(1)}, bf16[128,3584]{1,0:T(8,128)(2,1)}, u32[]{:S(2)}) copy-start(bf16[128,3584]{1,0:T(8,128)(2,1)} %gate_weight.1) | copy-start | bytes 2752516
  35.9 9.4 %copy-start.4 = (bf16[8,128]{1,0:T(8,128)(2,1)S(1)}, bf16[8,128]{1,0:T(8,128)(2,1)}, u32[]{:S(2)}) copy-start(bf16[8,128]{1,0:T(8,128)(2,1)} %residual.1) | copy-start | bytes 6148
  45.6 32.3 %copy-start.2 = (bf16[3584,128]{1,0:T(8,128)(2,1)S(1)}, bf16[3584,128]{1,0:T(8,128)(2,1)}, u32[]{:S(2)}) copy-start(bf16[3584,128]{1,0:T(8,128)(2,1)} %weight.3) | copy-start | bytes 2752516
